TPU v7x, 32 devices: a whole 2x2x4 slice. The times are simulated.
32 devices in a mesh: row: 8 (over z, core), col: 4 (over y, x).
Axes of the slice: x: 2, y: 2, z: 4, core: 2. Of those that a mesh axis runs over, the one named last changes fastest.
Arguments:
- inputs: bfloat16 [4096, 18432], P('col', 'row'), may hold values from -6 to 6
- out_grads: bfloat16 [4096, 18432], P('row', 'col'), may hold values from -0.09375 to 0.09375
- range_test: float32 [18432, 128], P('col'), may hold values from -0.046875 to 0.046875
- corange_test: float32 [256, 18432], P(None, 'row'), may hold values from -0.046875 to 0.046875
Outputs:
- range_sketch: float32 [18432, 128], P('row')
- corange_sketch: float32 [256, 18432], P(None, 'col')
- residual: float32 [18432, 18432], P('row', 'col')
All inputs are finite; a program needn't handle non-finite values.
Results may differ from a plain program's by a relative error of at most 0.0003.
Values may be sent and summed in bfloat16 or wider, within the bound.
No kernel may reach another device: no remote copies, remote signals or barrier semaphores. Data moves between devices by JAX's collectives and lax.ppermute only.
A program may use at most 192 MiB of HBM per device.

v0:
```python
import jax
import jax.numpy as jnp
from jax import lax
from jax.sharding import PartitionSpec as P

highest = lax.Precision.HIGHEST


def token_product(left_rows, right_rows):
    return lax.dot_general(
        left_rows, right_rows, (((0,), (0,)), ((), ())), preferred_element_type=jnp.float32
    )


def exact_product(left_side, right_side):
    return jnp.dot(left_side, right_side, precision=highest, preferred_element_type=jnp.float32)


def per_device(inputs, out_grads, range_test, corange_test):
    grads_all = lax.all_gather(out_grads, "row", axis=0, tiled=True)
    grads_range = exact_product(out_grads.astype(jnp.float32), range_test)
    grads_range = lax.psum(grads_range, "col")
    grads_range = lax.all_gather(grads_range, "row", axis=0, tiled=True)
    test_inputs = lax.dot_general(
        corange_test,
        inputs.astype(jnp.float32),
        (((1,), (1,)), ((), ())),
        precision=highest,
        preferred_element_type=jnp.float32,
    )
    test_inputs = lax.psum(test_inputs, "row")
    test_inputs = lax.all_gather(test_inputs, "col", axis=1, tiled=True)
    block_rows = lax.all_gather(inputs, "col", axis=0, tiled=True)
    new_gradient = token_product(block_rows, grads_all)
    new_range = lax.dot_general(
        block_rows.astype(jnp.float32),
        grads_range,
        (((0,), (0,)), ((), ())),
        precision=highest,
        preferred_element_type=jnp.float32,
    )
    new_corange = exact_product(test_inputs, grads_all.astype(jnp.float32))
    core_input = exact_product(test_inputs, grads_range)
    gram_matrix = lax.dot_general(
        core_input,
        core_input,
        (((0,), (0,)), ((), ())),
        precision=highest,
        preferred_element_type=jnp.float32,
    )
    factor_low = jnp.linalg.cholesky(gram_matrix)
    core_map = jax.scipy.linalg.cho_solve((factor_low, True), core_input.T)
    project = exact_product(core_map, new_corange)
    residual = new_gradient - exact_product(new_range, project)
    return (new_range, new_corange, residual)


def solution(mesh):
    placed = (P("col", "row"), P("row", "col"), P("col", None), P(None, "row"))
    return jax.shard_map(
        per_device,
        mesh=mesh,
        in_specs=placed,
        out_specs=(P("row", None), P(None, "col"), P("row", "col")),
        check_vma=False,
    )
```

profile of v0, /device:TPU:0, one launch (start us, length us, event | category | flops | bytes accessed | tf_op | source)
XLA Modules:
  0.0 899.8 jit_solution(7679866590538410267)
XLA Ops:
  7.2 0.0 copy-start
  7.2 0.0 all-reduce.3.cloned.1.call-start
  7.2 7.8 fusion.6
  15.0 0.0 all-reduce.3.cloned.1.call-update
  15.0 0.0 all-reduce.5.cloned.1.call-start
  15.1 0.0 copy-done
  15.1 7.2 fusion.8
  22.3 0.0 all-reduce.5.cloned.1.call-update
  22.3 0.0 all-gather.5.cloned.1.call-start
  22.3 38.5 %all-reduce.3.cloned.1.call-done = f32[512,128]{1,0:T(8,128)} async-done(((f32[512,128]{1,0:T(8,128)}), f32[512,128]{1,0:T(8,128)}) %all-reduce.3.cloned.1.call-update) | async-done | bytes 262160 | tf_op jit(solution)/shard_map/psum | solution.py:22
  60.8 0.0 all-gather.5.cloned.1.call-update
  60.8 0.0 all-gather.9.cloned.1.call-start
  60.9 61.8 %all-reduce.5.cloned.1.call-done = f32[256,1024]{1,0:T(8,128)} async-done(((f32[256,1024]{1,0:T(8,128)}), f32[256,1024]{1,0:T(8,128)}) %all-reduce.5.cloned.1.call-update) | async-done | bytes 1048592 | tf_op jit(solution)/shard_map/psum | solution.py:31
  122.7 0.0 all-gather.9.cloned.1.call-update
  122.7 0.0 all-gather.7.cloned.1.call-start
  122.8 0.5 all-gather.7.cloned.1.call-update
  123.3 0.2 all-gather.11.cloned.1.call-start
  123.5 0.3 all-gather.11.cloned.1.call-update
  123.9 28.6 %all-gather.5.cloned.1.call-done = f32[4096,128]{1,0:T(8,128)} async-done(((f32[512,128]{1,0:T(8,128)}), f32[4096,128]{1,0:T(8,128)}) %all-gather.5.cloned.1.call-update) | async-done | bytes 2097168 | tf_op jit(solution)/shard_map/all_gather | solution.py:23
  152.5 0.0 copy-start.2
  152.5 54.1 %all-gather.9.cloned.1.call-done = f32[256,4096]{1,0:T(8,128)} async-done(((f32[256,1024]{1,0:T(8,128)}), f32[256,4096]{1,0:T(8,128)}) %all-gather.9.cloned.1.call-update) | async-done | bytes 4194320 | tf_op jit(solution)/shard_map/all_gather | solution.py:32
  206.6 6.5 fusion.11
  213.1 0.4 fusion.12
  213.5 0.1 copy.7
  213.6 11.7 %cholesky.16 = f32[128,128]{1,0:T(8,128)S(1)} custom-call(f32[128,128]{1,0:T(8,128)S(1)} %fusion.5), custom_call_target="Cholesky" | custom-call | tf_op jit(solution)/shard_map/jit(cholesky)/cholesky | solution.py:51
  225.4 0.6 compare_reduce_fusion
  226.0 0.7 fusion
  226.7 9.8 %custom-call.10 = f32[1,128,128]{1,2,0:T(8,128)S(1)} custom-call(f32[1,128,128]{2,1,0:T(8,128)S(1)} %fusion), custom_call_target="InvertDiagBlocksLowerTriangular" | custom-call | tf_op jit(solution)/shard_map/jit(_cho_solve)/triangular_solve | solution.py:52
  236.5 0.3 fusion.3
  236.8 0.3 fusion.1
  237.1 147.5 %all-gather.7.cloned.1.call-done = bf16[4096,2304]{1,0:T(8,128)(2,1)} async-done(((bf16[1024,2304]{1,0:T(8,128)(2,1)}), bf16[4096,2304]{1,0:T(8,128)(2,1)}) %all-gather.7.cloned.1.call-update) | async-done | bytes 18874384 | tf_op jit(solution)/shard_map/all_gather | solution.py:33
  384.5 0.0 copy-done.2
  384.5 12.8 %fusion.7 = f32[128,2304]{1,0:T(8,128)S(1)} fusion(f32[4096,128]{1,0:T(8,128)S(1)} %copy-done.2, bf16[4096,2304]{1,0:T(8,128)(2,1)} %all-gather.7.cloned.1.call-done), kind=kOutput, calls=%fused_computation.14 | convolution fusion | flops 14495514624 | bytes 22151168 | tf_op jit(solution)/shard_map/dot_general | solution.py:35
  397.3 1.4 copy.8
  398.7 312.0 %all-gather.11.cloned.1.call-done = bf16[4096,4608]{1,0:T(8,128)(2,1)} async-done(((bf16[512,4608]{1,0:T(8,128)(2,1)}), bf16[4096,4608]{1,0:T(8,128)(2,1)}) %all-gather.11.cloned.1.call-update) | async-done | bytes 37748752 | tf_op jit(solution)/shard_map/all_gather | solution.py:20
  710.7 35.0 %fusion.9 = f32[256,4608]{1,0:T(8,128)S(1)} fusion(f32[256,4096]{1,0:T(8,128)} %all-gather.9.cloned.1.call-done, bf16[4096,4608]{1,0:T(8,128)(2,1)} %all-gather.11.cloned.1.call-done), kind=kOutput, calls=%fused_computation.16 | convolution fusion | flops 57982058496 | bytes 46661632 | tf_op jit(solution)/shard_map/dot_general | solution.py:16
  745.7 0.0 copy-start.3
  745.7 2.2 copy-done.3
  747.9 4.0 fusion.13
  751.9 98.9 %fusion.10 = f32[2304,4608]{1,0:T(8,128)} fusion(bf16[4096,2304]{1,0:T(8,128)(2,1)} %all-gather.7.cloned.1.call-done, bf16[4096,4608]{1,0:T(8,128)(2,1)} %all-gather.11.cloned.1.call-done), kind=kOutput, calls=%fused_computation.17 | convolution fusion | flops 86973087744 | bytes 99090432 | tf_op jit(solution)/shard_map/dot_general | solution.py:10
  850.9 0.0 copy-start.1
  850.9 41.6 %convolution_subtract_fusion = f32[2304,4608]{1,0:T(8,128)} fusion(f32[2304,4608]{1,0:T(8,128)} %fusion.10, f32[128,2304]{1,0:T(8,128)S(1)} %fusion.7, f32[128,4608]{1,0:T(8,128)} %fusion.13), kind=kOutput, calls=%fused_computation | convolution fusion | flops 16318070784 | bytes 88473600 | tf_op jit(solution)/shard_map/dot_general | solution.py:16
  892.5 0.0 copy-done.1
  (2 shorter events, 0.0 us)
Async XLA Ops:
  7.2 7.9 copy-start
  7.2 53.6 %all-reduce.3.cloned.1.call-start = ((), (), s32[]{:S(2)}) async-start(), calls=%async_computation | async-start | bytes 524288 | tf_op jit(solution)/shard_map/psum | solution.py:22
  15.0 107.7 %all-reduce.5.cloned.1.call-start = ((), (), s32[]{:S(2)}) async-start(), calls=%async_computation.3 | async-start | bytes 2097152 | tf_op jit(solution)/shard_map/psum | solution.py:31
  22.3 130.2 %all-gather.5.cloned.1.call-start = ((), (), s32[]{:S(2)}) async-start(), calls=%async_computation.1 | async-start | bytes 2359296 | tf_op jit(solution)/shard_map/all_gather | solution.py:23
  60.8 145.7 %all-gather.9.cloned.1.call-start = ((), (), s32[]{:S(2)}) async-start(), calls=%async_computation.4 | async-start | bytes 5242880 | tf_op jit(solution)/shard_map/all_gather | solution.py:32
  122.7 261.8 %all-gather.7.cloned.1.call-start = ((), (), s32[]{:S(2)}) async-start(), calls=%async_computation.2 | async-start | bytes 23592960 | tf_op jit(solution)/shard_map/all_gather | solution.py:33
  123.3 587.4 %all-gather.11.cloned.1.call-start = ((), (), s32[]{:S(2)}) async-start(), calls=%async_computation.5 | async-start | bytes 42467328 | tf_op jit(solution)/shard_map/all_gather | solution.py:20
  152.5 232.0 %copy-start.2 = (f32[4096,128]{1,0:T(8,128)S(1)}, f32[4096,128]{1,0:T(8,128)}, u32[]{:S(2)}) copy-start(f32[4096,128]{1,0:T(8,128)} %all-gather.5.cloned.1.call-done) | copy-start | bytes 6291460
  745.7 2.2 copy-start.3
  850.9 41.6 %copy-start.1 = (f32[256,2304]{1,0:T(8,128)S(1)}, f32[256,2304]{1,0:T(8,128)}, u32[]{:S(2)}) copy-start(f32[256,2304]{1,0:T(8,128)} %param.7) | copy-start | bytes 7077892
Sparse Core Ops, SparseCore 0:
  15.2 45.6 all-reduce.2
  63.9 58.8 all-reduce.4
  124.4 28.0 all-gather.4
  154.4 52.1 all-gather.8
  208.4 176.0 all-gather.6
  386.1 324.5 all-gather.10
where the time goes:
time: 906 us; the launch traced here: 900 us
  waiting for transfers between devices  643 us (71%)
  matrix products  215 us (24%)
  other arithmetic  22.9 us (3%)
  between operations  14.7 us (2%)
    all_gather x1, waiting for transfers between devices, per_device(): grads_all = lax.all_gather(out_grads, 'row', axis=0, tiled=True)  312 us
    all_gather x1, waiting for transfers between devices, per_device(): block_rows = lax.all_gather(inputs, 'col', axis=0, tiled=True)  147 us
    dot_general x1, matrix products, token_product(): lax.dot_general(left_rows, right_rows, (((0,), (0,)), ((), ())), preferre...  98.9 us
    dot_general x5, matrix products, exact_product(): jnp.dot(left_side, right_side, precision=highest, preferred_element_type=...  94.9 us
    psum x1, waiting for transfers between devices, per_device(): test_inputs = lax.psum(test_inputs, 'row')  61.8 us
    all_gather x1, waiting for transfers between devices, per_device(): test_inputs = lax.all_gather(test_inputs, 'col', axis=1, tiled=True)  54.1 us
    psum x1, waiting for transfers between devices, per_device(): grads_range = lax.psum(grads_range, 'col')  38.5 us
    all_gather x1, waiting for transfers between devices, per_device(): grads_range = lax.all_gather(grads_range, 'row', axis=0, tiled=True)  28.6 us
  transfers between devices with their start and end apart: 6, of which 6 were waited for; matrix products, arithmetic and copies ran while one was open for 6% of the time, Pallas kernels for 0%

commit v1 on v0

v1 whole, which is shorter than its diff:
```python
import math

import jax
import jax.numpy as jnp
from jax import lax
from jax.experimental import pallas as pl
from jax.experimental.pallas import tpu as pltpu
from jax.sharding import Mesh, PartitionSpec as P

highest = lax.Precision.HIGHEST
ROW = ("z", "core")
COL = ("a", "b")
VMEM_BYTES = 60 << 20


def exact_product(left, right, dims):
    return lax.dot_general(
        left, right, (dims, ((), ())), precision=highest, preferred_element_type=jnp.float32
    )


def split_two(array):
    high = array.astype(jnp.bfloat16)
    low = (array - high.astype(jnp.float32)).astype(jnp.bfloat16)
    return high, low


def largest_tile(size, limit):
    fits = [t for t in range(128, limit + 1, 128) if size % t == 0]
    return fits[-1] if fits else size


def shifted(array, axes, size, by):
    return lax.ppermute(array, axes, [(i, (i + by) % size) for i in range(size)])


def turn(array, after):
    rows, columns = array.shape
    half = rows // 2
    tile = largest_tile(columns, 384)

    def kernel(array_ref, *refs):
        refs[-2][...] = array_ref[:half, :].T
        refs[-1][...] = array_ref[half:, :].T

    return pl.pallas_call(
        kernel,
        grid=(columns // tile,),
        in_specs=[pl.BlockSpec((rows, tile), lambda i: (0, i))]
        + [pl.BlockSpec(memory_space=pl.ANY)] * len(after),
        out_specs=[pl.BlockSpec((tile, half), lambda i: (i, 0))] * 2,
        out_shape=[jax.ShapeDtypeStruct((columns, half), array.dtype)] * 2,
        compiler_params=pltpu.CompilerParams(vmem_limit_bytes=VMEM_BYTES),
    )(array, *after)


def gather_tokens(halves, sizes, index):
    near, far, near_starts, far_starts = [], [], [], []
    half = halves[0].shape[1]
    for part, start in enumerate(halves):
        order = (1, 0) if part == 0 else (0, 1)
        first, second = (COL[axis] for axis in order)
        size_first, size_second = (sizes[axis] for axis in order)

        def token(by_first, by_second):
            by = (by_second, by_first) if part == 0 else (by_first, by_second)
            at = [lax.rem(index[n] - by[n] + sizes[n], sizes[n]) for n in range(2)]
            return ((at[0] * sizes[1] + at[1]) * 2 + part) * half

        line = gathered_parts(start, first, size_first)
        near.append(line)
        near_starts += [token(by, 0) for by in range(size_first)]
        for by_second in range(1, size_second):
            far.append(shifted(line, second, size_second, by_second))
            far_starts += [token(by, by_second) for by in range(size_first)]
    return near, far, near_starts + far_starts


def scattered(parts, axes, size, index):
    terms = [lax.dynamic_index_in_dim(parts, index, 0, keepdims=False)]
    for by in range(1, size):
        target = lax.rem(index + by, size)
        sent = lax.dynamic_index_in_dim(parts, target, 0, keepdims=False)
        terms.append(shifted(sent, axes, size, by))
    return terms


def gathered_parts(own, axes, size):
    return jnp.concatenate([own] + [shifted(own, axes, size, by) for by in range(1, size)], axis=0)


def combine(left_terms, right_terms, after):
    count = len(left_terms)
    rank = left_terms[0].shape[1]
    unit, rank_z = right_terms[0].shape
    terms = list(left_terms) + list(right_terms)

    def kernel(*refs):
        ins, out_ref = refs[: len(terms)], refs[-1]
        left = ins[0][...]
        for ref in ins[1:count]:
            left += ref[...]
        right = ins[count][...]
        for ref in ins[count + 1 :]:
            right += ref[...]
        out_ref[:, :rank] = left
        out_ref[:, rank:] = right

    whole = pl.BlockSpec(memory_space=pltpu.VMEM)
    return pl.pallas_call(
        kernel,
        in_specs=[whole] * len(terms) + [pl.BlockSpec(memory_space=pl.ANY)] * len(after),
        out_specs=whole,
        out_shape=jax.ShapeDtypeStruct((unit, rank + rank_z), jnp.float32),
        compiler_params=pltpu.CompilerParams(vmem_limit_bytes=VMEM_BYTES),
    )(*terms, *after)


def finish(stacks, range_starts, test_starts, rank, after):
    rank_z = stacks[0].shape[1] - rank
    blocks = range_starts.shape[0] // len(stacks)
    tokens = stacks[0].shape[0] * len(stacks)
    unit = stacks[0].shape[0] // blocks
    step = largest_tile(tokens, 128)

    def kernel(range_starts_ref, test_starts_ref, *refs):
        ins = refs[: len(stacks)]
        parts_ref, high_ref, low_ref, core_ref, range_ref, test_ref = refs[-6:]
        for k, stack in enumerate(ins):

            @pl.loop(0, blocks)
            def _(i):
                rows = pl.ds(pl.multiple_of(i * unit, unit), unit)
                to = pl.multiple_of(range_starts_ref[k * blocks + i], unit)
                range_ref[pl.ds(to, unit), :] = stack[rows, :rank]
                to = pl.multiple_of(test_starts_ref[k * blocks + i], unit)
                test_ref[pl.ds(to, unit), :] = stack[rows, rank:]

        high, low = split_two(range_ref[...])
        parts_ref[:, :rank] = high
        parts_ref[:, rank:] = low
        for at in range(0, tokens, step):
            high, low = split_two(test_ref[at : at + step, :].T)
            high_ref[:, at : at + step] = high
            low_ref[:, at : at + step] = low
        core_ref[...] = lax.dot_general(
            test_ref[...],
            range_ref[...],
            (((0,), (0,)), ((), ())),
            precision=highest,
            preferred_element_type=jnp.float32,
        )

    whole = pl.BlockSpec(memory_space=pltpu.VMEM)
    return pl.pallas_call(
        kernel,
        grid_spec=pltpu.PrefetchScalarGridSpec(
            num_scalar_prefetch=2,
            grid=(),
            in_specs=[whole] * len(stacks) + [pl.BlockSpec(memory_space=pl.ANY)] * len(after),
            out_specs=[whole] * 4,
            scratch_shapes=[
                pltpu.VMEM((tokens, rank), jnp.float32),
                pltpu.VMEM((tokens, rank_z), jnp.float32),
            ],
        ),
        out_shape=[
            jax.ShapeDtypeStruct((tokens, 2 * rank), jnp.bfloat16),
            jax.ShapeDtypeStruct((rank_z, tokens), jnp.bfloat16),
            jax.ShapeDtypeStruct((rank_z, tokens), jnp.bfloat16),
            jax.ShapeDtypeStruct((rank_z, rank), jnp.float32),
        ],
        compiler_params=pltpu.CompilerParams(vmem_limit_bytes=VMEM_BYTES),
    )(range_starts, test_starts, *stacks, *after)


def assemble(stacks, starts, test_parts):
    starts = jnp.stack(starts).astype(jnp.int32)
    width = stacks[0].shape[1]
    tokens = test_parts.shape[0]
    rows = sum(stack.shape[0] for stack in stacks) * width // tokens
    rank = test_parts.shape[1] // 2
    tile = largest_tile(rows, 384)
    arrays, specs = [], []
    for stack in stacks:
        for place in range(stack.shape[0] // rows):
            first = place * (rows // tile)
            arrays.append(stack)
            specs.append(pl.BlockSpec((tile, width), lambda i, s, first=first: (first + i, 0)))

    def kernel(starts_ref, *refs):
        ins, test_ref = refs[: len(arrays)], refs[len(arrays)]
        all_ref, sketch_ref, split_ref = refs[-3:]
        for k, piece in enumerate(ins):
            all_ref[:, pl.ds(pl.multiple_of(starts_ref[k], width), width)] = piece[...]
        both = jnp.dot(all_ref[...], test_ref[...], preferred_element_type=jnp.float32)
        sketch = both[:, :rank] + both[:, rank:]
        sketch_ref[...] = sketch
        high, low = split_two(sketch)
        split_ref[:, :rank] = high
        split_ref[:, rank : 2 * rank] = low
        split_ref[:, 2 * rank :] = high

    return pl.pallas_call(
        kernel,
        grid_spec=pltpu.PrefetchScalarGridSpec(
            num_scalar_prefetch=1,
            grid=(rows // tile,),
            in_specs=specs + [pl.BlockSpec((tokens, 2 * rank), lambda i, s: (0, 0))],
            out_specs=[
                pl.BlockSpec((tile, tokens), lambda i, s: (i, 0)),
                pl.BlockSpec((tile, rank), lambda i, s: (i, 0)),
                pl.BlockSpec((tile, 3 * rank), lambda i, s: (i, 0)),
            ],
        ),
        out_shape=[
            jax.ShapeDtypeStruct((rows, tokens), jnp.bfloat16),
            jax.ShapeDtypeStruct((rows, rank), jnp.float32),
            jax.ShapeDtypeStruct((rows, 3 * rank), jnp.bfloat16),
        ],
        compiler_params=pltpu.CompilerParams(vmem_limit_bytes=VMEM_BYTES),
        cost_estimate=pl.CostEstimate(
            flops=4 * rows * tokens * rank, bytes_accessed=4 * rows * tokens, transcendentals=0
        ),
    )(starts, *arrays, test_parts)


def slab(rows_all, grads, sketch_split, test_high, test_low, core_map, first, block, columns, before):
    rows, tokens = rows_all.shape
    width = grads.shape[1]
    rank, rank_z = core_map.shape
    tile = largest_tile(rows, 768)
    at = first // block

    def kernel(rows_ref, grads_ref, split_ref, high_ref, low_ref, map_ref, *refs):
        corange_ref, residual_ref, project_ref = refs[-3:]

        @pl.when(pl.program_id(1) == 0)
        def _():
            corange = jnp.dot(high_ref[...], grads_ref[...], preferred_element_type=jnp.float32)
            corange += jnp.dot(low_ref[...], grads_ref[...], preferred_element_type=jnp.float32)
            corange_ref[...] = corange
            project = -jnp.dot(
                map_ref[...], corange, precision=highest, preferred_element_type=jnp.float32
            )
            high, low = split_two(project)
            project_ref[:rank, :] = high
            project_ref[rank : 2 * rank, :] = high
            project_ref[2 * rank :, :] = low

        residual_ref[...] = jnp.dot(
            rows_ref[...], grads_ref[...], preferred_element_type=jnp.float32
        ) + jnp.dot(split_ref[...], project_ref[...], preferred_element_type=jnp.float32)

    in_specs = [
        pl.BlockSpec((tile, tokens), lambda j, i: (i, 0)),
        pl.BlockSpec((tokens, block), lambda j, i: (0, j)),
        pl.BlockSpec((tile, 3 * rank), lambda j, i: (i, 0)),
        pl.BlockSpec((rank_z, tokens), lambda j, i: (0, 0)),
        pl.BlockSpec((rank_z, tokens), lambda j, i: (0, 0)),
        pl.BlockSpec((rank, rank_z), lambda j, i: (0, 0)),
    ] + [pl.BlockSpec(memory_space=pl.ANY)] * len(before)
    return pl.pallas_call(
        kernel,
        grid=(width // block, rows // tile),
        in_specs=in_specs,
        out_specs=[
            pl.BlockSpec((rank_z, block), lambda j, i: (0, at + j)),
            pl.BlockSpec((tile, block), lambda j, i: (i, at + j)),
        ],
        out_shape=[
            jax.ShapeDtypeStruct((rank_z, columns), jnp.float32),
            jax.ShapeDtypeStruct((rows, columns), jnp.float32),
        ],
        scratch_shapes=[pltpu.VMEM((3 * rank, block), jnp.bfloat16)],
        input_output_aliases={6: 0, 7: 1} if before else {},
        compiler_params=pltpu.CompilerParams(vmem_limit_bytes=VMEM_BYTES),
        cost_estimate=pl.CostEstimate(
            flops=2 * width * (rows * (tokens + 3 * rank) + 2 * rank_z * tokens),
            bytes_accessed=4 * rows * width + 2 * tokens * (rows + width),
            transcendentals=0,
        ),
    )(rows_all, grads, sketch_split, test_high, test_low, core_map, *before)


def slices_of(columns):
    unit = largest_tile(columns, 512)
    count = columns // unit
    last = max(1, count // 9)
    middle = max(1, 2 * count // 9)
    slices, first = [], 0
    for n in (count - middle - last, middle, last):
        if n > 0:
            twice = n % 2 == 0 and first % (2 * unit) == 0
            slices.append((first, n * unit, 2 * unit if twice else unit))
            first += n * unit
    return slices


def solution(mesh):
    size_row, size_col = mesh.shape["row"], mesh.shape["col"]
    size_b = next(n for n in range(math.isqrt(size_col), size_col + 1) if size_col % n == 0)
    size_a = size_col // size_b
    size_core = 2 if size_row % 2 == 0 else 1
    size_z = size_row // size_core
    finer = Mesh(mesh.devices.reshape(size_z, size_core, size_a, size_b), ROW + COL)

    def per_device(inputs, out_grads, range_test, corange_test):
        z, core = lax.axis_index("z"), lax.axis_index("core")
        a, b = lax.axis_index("a"), lax.axis_index("b")
        col = a * size_b + b
        columns = out_grads.shape[1]
        rank, rank_z = range_test.shape[1], corange_test.shape[0]

        gathered = []
        for first, width, block in slices_of(columns):
            part = out_grads[:, first : first + width]
            gathered.append((first, block, lax.all_gather(part, ROW, axis=0, tiled=True)))

        grads_range = exact_product(out_grads.astype(jnp.float32), range_test, ((1,), (0,)))
        test_inputs = exact_product(inputs.astype(jnp.float32), corange_test, ((1,), (1,)))
        tokens = inputs.shape[0] * size_col
        unit = inputs.shape[0] // size_row
        range_terms = scattered(grads_range.reshape(size_col, unit, rank), COL, size_col, col)
        halves = turn(inputs, range_terms)
        near, far, starts = gather_tokens(halves, (size_a, size_b), (a, b))
        test_inputs = test_inputs.reshape(size_z, size_core, unit, rank_z).transpose(1, 0, 2, 3)
        test_inputs = sum(scattered(test_inputs, "core", size_core, core))
        test_terms = scattered(test_inputs, "z", size_z, z)
        own = combine(range_terms, test_terms, near)
        own = gathered_parts(own, "z", size_z)
        own = gathered_parts(own, COL, size_col)
        stacks = [own] + [shifted(own, "core", size_core, by) for by in range(1, size_core)]
        at_core = lax.rem(core - jnp.arange(size_core) + size_core, size_core)[:, None, None]
        at_col = lax.rem(col - jnp.arange(size_col) + size_col, size_col)[None, :, None]
        at_z = lax.rem(z - jnp.arange(size_z) + size_z, size_z)[None, None, :]
        at_row = at_z * size_core + at_core
        range_starts = (at_row * size_col + at_col) * unit
        test_starts = (at_col * size_row + at_row) * unit
        range_parts, test_high, test_low, core_input = finish(
            stacks,
            range_starts.reshape(-1).astype(jnp.int32),
            test_starts.reshape(-1).astype(jnp.int32),
            rank,
            [],
        )

        gram_matrix = exact_product(core_input, core_input, ((0,), (0,)))
        factor_low = jnp.linalg.cholesky(gram_matrix)
        core_map = jax.scipy.linalg.cho_solve((factor_low, True), core_input.T)

        rows_all, new_range, sketch_split = assemble(near + far, starts, range_parts)

        out = ()
        for first, block, grads in gathered:
            out = slab(
                rows_all, grads, sketch_split, test_high, test_low, core_map, first, block, columns, out
            )
        return (new_range, out[0], out[1])

    return jax.shard_map(
        per_device,
        mesh=finer,
        in_specs=(P(COL, ROW), P(ROW, COL), P(COL, None), P(None, ROW)),
        out_specs=(P(ROW, None), P(None, COL), P(ROW, COL)),
        check_vma=False,
    )
```

time: 906 us -> 457 us (0.50)
  the two profiles are of different devices: /device:TPU:0 before, /device:TPU:26 now
where the time goes in v1:
time: 457 us; the launch traced here: 451 us
  Pallas kernels  184 us (40%)
  waiting for transfers between devices  162 us (35%)
  local copies, waits for them, and re-layouts  31.5 us (7%)
  other arithmetic  25.2 us (6%)
  starting transfers between devices  17.1 us (4%)
  matrix products  15.9 us (3%)
  between operations  14.4 us (3%)
    ppermute x18, waiting for transfers between devices, shifted(): lax.ppermute(array, axes, [(i, (i + by) % size) for i in range(size)])  162 us
    pallas_call x3, Pallas kernels, slab(): pl.pallas_call(kernel, grid=(width // block, rows // tile), in_specs=in_s...  148 us
    ppermute x18, starting transfers between devices, shifted(): lax.ppermute(array, axes, [(i, (i + by) % size) for i in range(size)])  17 us
    pallas_call x1, Pallas kernels, assemble(): pl.pallas_call(kernel, grid_spec=pltpu.PrefetchScalarGridSpec(num_scalar_...  16.7 us
    dot_general x3, matrix products, exact_product(): lax.dot_general(left, right, (dims, ((), ())), precision=highest, preferr...  13.8 us
    another operation x3, other arithmetic, per_device(): factor_low = jnp.linalg.cholesky(gram_matrix)  12.4 us
    unnamed x26, local copies, waits for them, and re-layouts  12 us
    pallas_call x1, Pallas kernels, finish(): pl.pallas_call(kernel, grid_spec=pltpu.PrefetchScalarGridSpec(num_scalar_...  10.8 us
  transfers between devices with their start and end apart: 21, of which 11 were waited for; matrix products, arithmetic and copies ran while one was open for 15% of the time, Pallas kernels for 36%

profile of v1, /device:TPU:26, one launch (start us, length us, event | category | flops | bytes accessed | tf_op | source)
XLA Modules:
  0.0 450.8 jit_solution(8058651869496523474)
XLA Ops:
  7.2 3.9 slice.29
  11.2 2.3 slice.28
  13.6 6.5 %fusion.10 = f32[512,128]{1,0:T(8,128)S(1)} fusion(bf16[512,4608]{1,0:T(8,128)(2,1)} %param.5, f32[4608,128]{1,0:T(8,128)} %param.6), kind=kOutput, calls=%fused_computation.49 | convolution fusion | flops 3623878656 | bytes 7340032 | tf_op jit(solution)/shard_map/dot_general | solution.py:17
  20.8 1.5 collective-permute-start
  22.8 1.5 collective-permute-start.2
  25.1 2.0 collective-permute-done.1.refs_2_
  27.1 0.8 collective-permute-done.2.refs_3_
  28.6 6.4 %shard_map.67 = (bf16[2304,512]{1,0:T(8,128)(2,1)}, bf16[2304,512]{1,0:T(8,128)(2,1)}) custom-call(bf16[1024,2304]{1,0:T(8,128)(2,1)} %array_ref.1, f32[128,128]{1,0:T(8,128)} %get-tuple-element.40.refs_0_, f32[128,128]{1,0:T(8,128)} %copy-done.3, f32[128,128]{1,0:T(8,128)} %copy-done.4, f32[128,128]{1,0:T(8,128)} %copy-done.5), custom_call_target="tpu_custom_call" | custom-call | tf_op jit(solution)/shard_map/pallas_call | solution.py:46
  35.0 1.5 collective-permute-start.4
  36.5 5.9 %fusion.11 = f32[1024,256]{1,0:T(8,128)S(1)} fusion(bf16[1024,2304]{1,0:T(8,128)(2,1)} %array_ref.1, f32[256,2304]{1,0:T(8,128)S(1)} %copy-done), kind=kOutput, calls=%fused_computation.50 | convolution fusion | flops 7247757312 | bytes 8126464 | tf_op jit(solution)/shard_map/dot_general | solution.py:17
  42.4 0.8 dynamic-slice_bitcast_fusion
  43.2 3.4 constant_dynamic-update-slice_fusion.3
  46.7 1.6 constant_dynamic-update-slice_fusion.1
  48.2 1.1 bitcast_add_fusion
  50.5 3.3 collective-permute-start.8
  53.9 33.3 %collective-permute-done.4 = bf16[2304,512]{1,0:T(8,128)(2,1)} collective-permute-done((bf16[2304,512]{1,0:T(8,128)(2,1)}, bf16[2304,512]{1,0:T(8,128)(2,1)}, u32[]{:S(2)}, u32[]{:S(2)}) %collective-permute-start.4) | collective-permute-done | bytes 2359328 | tf_op jit(solution)/shard_map/ppermute | solution.py:34
  87.2 3.2 constant_dynamic-update-slice_fusion.2.refs_9_.refs_2_.refs_3_
  90.4 3.2 constant_dynamic-update-slice_fusion.refs_8_.refs_0_.refs_1_
  94.4 1.9 shard_map.68
  96.5 2.0 collective-permute-start.12
  98.7 11.9 %collective-permute-done.11 = f32[128,384]{1,0:T(8,128)S(1)} collective-permute-done((f32[128,384]{1,0:T(8,128)}, f32[128,384]{1,0:T(8,128)S(1)}, u32[]{:S(2)}, u32[]{:S(2)}) %collective-permute-start.11) | collective-permute-done | bytes 196640 | tf_op jit(solution)/shard_map/ppermute | solution.py:34
  110.6 31.0 %collective-permute-done.12 = f32[128,384]{1,0:T(8,128)S(1)} collective-permute-done((f32[128,384]{1,0:T(8,128)}, f32[128,384]{1,0:T(8,128)S(1)}, u32[]{:S(2)}, u32[]{:S(2)}) %collective-permute-start.12) | collective-permute-done | bytes 196640 | tf_op jit(solution)/shard_map/ppermute | solution.py:34
  141.5 1.0 pad_maximum_fusion
  142.5 1.2 collective-permute-start.14
  143.7 0.9 collective-permute-start.15
  144.6 1.2 collective-permute-start.16
  145.7 1.6 collective-permute-start.6
  147.3 0.9 collective-permute-start.5
  148.2 1.6 constant_dynamic-update-slice_fusion.10
  151.9 11.1 %collective-permute-done.14 = f32[512,384]{1,0:T(8,128)S(1)} collective-permute-done((f32[512,384]{1,0:T(8,128)S(1)}, f32[512,384]{1,0:T(8,128)S(1)}, u32[]{:S(2)}, u32[]{:S(2)}) %collective-permute-start.14) | collective-permute-done | bytes 786464 | tf_op jit(solution)/shard_map/ppermute | solution.py:34
  163.0 1.0 constant_dynamic-update-slice_fusion.6
  164.0 17.0 %collective-permute-done.15 = f32[512,384]{1,0:T(8,128)S(1)} collective-permute-done((f32[512,384]{1,0:T(8,128)S(1)}, f32[512,384]{1,0:T(8,128)S(1)}, u32[]{:S(2)}, u32[]{:S(2)}) %collective-permute-start.15) | collective-permute-done | bytes 786464 | tf_op jit(solution)/shard_map/ppermute | solution.py:34
  181.0 0.9 constant_dynamic-update-slice_fusion.5
  182.0 1.0 constant_dynamic-update-slice_fusion.4.refs_0_
  182.9 1.9 slice.27
  186.9 2.0 collective-permute-done.17.refs_1_
  188.9 10.8 %shard_map.69 = (bf16[4096,256]{1,0:T(8,128)(2,1)}, bf16[256,4096]{1,0:T(8,128)(2,1)}, bf16[256,4096]{1,0:T(8,128)(2,1)}, f32[256,128]{1,0:T(8,128)}) custom-call(s32[32]{0:T(128)} %mul.111.range_starts_ref, s32[32]{0:T(128)} %mul.114.test_starts_ref, f32[2048,384]{1,0:T(8,128)} %constant_dynamic-update-slice_fusion.4.refs_0_, ...), custom_call_target="tpu_custom_call" | custom-call | tf_op jit(solution)/shard_map/pallas_call | solution.py:155
  199.7 1.4 fusion.12
  201.2 11.7 %cholesky.16 = f32[128,128]{1,0:T(8,128)S(1)} custom-call(f32[128,128]{1,0:T(8,128)S(1)} %fusion.5), custom_call_target="Cholesky" | custom-call | tf_op jit(solution)/shard_map/jit(cholesky)/cholesky | solution.py:349
  214.2 9.8 %custom-call.10 = f32[1,128,128]{1,2,0:T(8,128)S(1)} custom-call(f32[1,128,128]{2,1,0:T(8,128)S(1)} %fusion), custom_call_target="InvertDiagBlocksLowerTriangular" | custom-call | tf_op jit(solution)/shard_map/jit(_cho_solve)/triangular_solve | solution.py:350
  224.0 1.2 fusion.3
  225.3 0.9 fusion.1.map_ref
  226.2 51.2 %collective-permute-done.6.refs_6_.refs_7_ = bf16[4608,512]{1,0:T(8,128)(2,1)} collective-permute-done((bf16[4608,512]{1,0:T(8,128)(2,1)}, bf16[4608,512]{1,0:T(8,128)(2,1)}, u32[]{:S(2)}, u32[]{:S(2)}) %collective-permute-start.6) | collective-permute-done | bytes 4718624 | tf_op jit(solution)/shard_map/ppermute | solution.py:34
  277.4 1.2 collective-permute-done.5.refs_4_.refs_5_
  278.6 16.7 %shard_map.70 = (bf16[2304,4096]{1,0:T(8,128)(2,1)}, f32[2304,128]{1,0:T(8,128)}, bf16[2304,384]{1,0:T(8,128)(2,1)}) custom-call(s32[8]{0:T(128)} %stack.35.starts_ref, bf16[4608,512]{1,0:T(8,128)(2,1)} %constant_dynamic-update-slice_fusion.refs_8_.refs_0_.refs_1_, bf16[4608,512]{1,0:T(8,128)(2,1)} %constant_dynamic-update-slice_fusion.refs_8_.refs_0_.refs_1_, ...), custom_call_target="tpu_custom_call" | custom-call | flops 4831838208 | bytes 37748736 | tf_op jit(solution)/shard_map/pallas_call | solution.py:204
  295.4 91.5 %shard_map.71 = (f32[256,4608]{1,0:T(8,128)}, f32[2304,4608]{1,0:T(8,128)}) custom-call(bf16[2304,4096]{1,0:T(8,128)(2,1)} %get-tuple-element.22.rows_ref, bf16[4096,3072]{1,0:T(8,128)(2,1)} %all-gather.8.cloned.1.call-done.grads_ref, bf16[2304,384]{1,0:T(8,128)(2,1)} %get-tuple-element.23.split_ref, bf16[256,4096]{1,0:T(8,128)(2,1)} %get-tuple-element.24.high_ref, ...), custom_call_target="tpu_custom_call" | custom-call | flops 76302778368 | bytes 72351744 | tf_op jit(solution)/shard_map/pallas_call | solution.py:263
  386.9 36.1 %shard_map.72 = (f32[256,4608]{1,0:T(8,128)}, f32[2304,4608]{1,0:T(8,128)}) custom-call(bf16[2304,4096]{1,0:T(8,128)(2,1)} %get-tuple-element.22.rows_ref, bf16[4096,1024]{1,0:T(8,128)(2,1)} %all-gather.6.cloned.1.call-done.grads_ref, bf16[2304,384]{1,0:T(8,128)(2,1)} %get-tuple-element.23.split_ref, ...), custom_call_target="tpu_custom_call", output_to_operand_aliasing={{0}: (6, {}), {1}: (7, {})} | custom-call | flops 25434259456 | bytes 36700160 | tf_op jit(solution)/shard_map/pallas_call | solution.py:263
  422.9 20.9 %shard_map.73 = (f32[256,4608]{1,0:T(8,128)}, f32[2304,4608]{1,0:T(8,128)}) custom-call(bf16[2304,4096]{1,0:T(8,128)(2,1)} %get-tuple-element.22.rows_ref, bf16[4096,512]{1,0:T(8,128)(2,1)} %all-gather.4.cloned.1.call-done.grads_ref, bf16[2304,384]{1,0:T(8,128)(2,1)} %get-tuple-element.23.split_ref, ...), custom_call_target="tpu_custom_call", output_to_operand_aliasing={{0}: (6, {}), {1}: (7, {})} | custom-call | flops 12717129728 | bytes 27787264 | tf_op jit(solution)/shard_map/pallas_call | solution.py:263
  (62 shorter events, 10.7 us)
Async XLA Ops:
  7.2 29.3 %copy-start = (f32[256,2304]{1,0:T(8,128)S(1)}, f32[256,2304]{1,0:T(8,128)}, u32[]{:S(2)}) copy-start(f32[256,2304]{1,0:T(8,128)} %param.7) | copy-start | bytes 7077892
  7.2 288.2 %all-gather.8.cloned.1.call-start = ((), (), s32[]{:S(2)}) async-start(), calls=%async_computation.2 | async-start | bytes 28311552 | tf_op jit(solution)/shard_map/all_gather | solution.py:318
  11.2 375.7 %all-gather.6.cloned.1.call-start = ((), (), s32[]{:S(2)}) async-start(), calls=%async_computation.1 | async-start | bytes 9437184 | tf_op jit(solution)/shard_map/all_gather | solution.py:318
  13.6 409.4 %all-gather.4.cloned.1.call-start = ((), (), s32[]{:S(2)}) async-start(), calls=%async_computation | async-start | bytes 4718592 | tf_op jit(solution)/shard_map/all_gather | solution.py:318
  20.8 4.3 collective-permute-start
  22.3 4.8 %collective-permute-start.1 = (f32[128,128]{1,0:T(8,128)S(1)}, f32[128,128]{1,0:T(8,128)S(1)}, u32[]{:S(2)}, u32[]{:S(2)}) collective-permute-start(f32[128,128]{1,0:T(8,128)S(1)} %get-tuple-element.38), channel_id=1, source_target_pairs={{0,2},{1,3},{2,0},{3,1},{4,6},{5,7},{6,4},{7,5},{8,10},{9,11},{10,... | collective-permute-start | bytes 196616 | tf_op jit(solution)/shard_map/ppermute | solution.py:34
  22.8 5.2 %collective-permute-start.2 = (f32[128,128]{1,0:T(8,128)S(1)}, f32[128,128]{1,0:T(8,128)S(1)}, u32[]{:S(2)}, u32[]{:S(2)}) collective-permute-start(f32[128,128]{1,0:T(8,128)S(1)} %get-tuple-element.37), channel_id=1, source_target_pairs={{0,3},{1,0},{2,1},{3,2},{4,7},{5,4},{6,5},{7,6},{8,11},{9,8},{10,9... | collective-permute-start | bytes 196616 | tf_op jit(solution)/shard_map/ppermute | solution.py:34
  25.1 2.9 copy-start.3
  27.1 0.9 copy-start.4
  28.0 0.6 copy-start.5
  35.0 52.2 %collective-permute-start.4 = (bf16[2304,512]{1,0:T(8,128)(2,1)}, bf16[2304,512]{1,0:T(8,128)(2,1)}, u32[]{:S(2)}, u32[]{:S(2)}) collective-permute-start(bf16[2304,512]{1,0:T(8,128)(2,1)} %get-tuple-element.19), channel_id=1, source_target_pairs={{0,2},{2,0},{1,3},{3,1},{4,6},{6,4},{5,7},{7,5},{8,10},{10,8},{9,1... | collective-permute-start | bytes 7077896 | tf_op jit(solution)/shard_map/ppermute | solution.py:34
  36.5 53.9 %collective-permute-start.3 = (bf16[2304,512]{1,0:T(8,128)(2,1)}, bf16[2304,512]{1,0:T(8,128)(2,1)}, u32[]{:S(2)}, u32[]{:S(2)}) collective-permute-start(bf16[2304,512]{1,0:T(8,128)(2,1)} %get-tuple-element.18), channel_id=1, source_target_pairs={{0,1},{1,0},{2,3},{3,2},{4,5},{5,4},{6,7},{7,6},{8,9},{9,8},{10,11... | collective-permute-start | bytes 7077896 | tf_op jit(solution)/shard_map/ppermute | solution.py:34
  42.4 4.3 copy-start.2
  43.2 5.0 %collective-permute-start.7 = (f32[4,128,256]{2,1,0:T(8,128)}, f32[4,128,256]{2,1,0:T(8,128)}, u32[]{:S(2)}, u32[]{:S(2)}) collective-permute-start(f32[4,128,256]{2,1,0:T(8,128)} %dynamic-slice_bitcast_fusion), channel_id=1, source_target_pairs={{0,4},{4,0},{1,5},{5,1},{2,6},{6,2},{3,7},{7,3},{8,12},{12,8},{9,1... | collective-permute-start | bytes 1572872 | tf_op jit(solution)/shard_map/ppermute | solution.py:34
  50.0 43.6 %collective-permute-start.10 = (f32[128,256]{1,0:T(8,128)S(1)}, f32[128,256]{1,0:T(8,128)S(1)}, u32[]{:S(2)}, u32[]{:S(2)}) collective-permute-start(f32[128,256]{1,0:T(8,128)S(1)} %get-tuple-element.33), channel_id=1, source_target_pairs={{0,24},{8,0},{16,8},{24,16},{1,25},{9,1},{17,9},{25,17},{2,26},{10... | collective-permute-start | bytes 393224 | tf_op jit(solution)/shard_map/ppermute | solution.py:34
  50.5 43.1 %collective-permute-start.8 = (f32[128,256]{1,0:T(8,128)S(1)}, f32[128,256]{1,0:T(8,128)S(1)}, u32[]{:S(2)}, u32[]{:S(2)}) collective-permute-start(f32[128,256]{1,0:T(8,128)S(1)} %get-tuple-element.35), channel_id=1, source_target_pairs={{0,8},{8,16},{16,24},{24,0},{1,9},{9,17},{17,25},{25,1},{2,10},{10... | collective-permute-start | bytes 393224 | tf_op jit(solution)/shard_map/ppermute | solution.py:34
  53.9 39.8 %collective-permute-start.9 = (f32[128,256]{1,0:T(8,128)S(1)}, f32[128,256]{1,0:T(8,128)S(1)}, u32[]{:S(2)}, u32[]{:S(2)}) collective-permute-start(f32[128,256]{1,0:T(8,128)S(1)} %get-tuple-element.34), channel_id=1, source_target_pairs={{0,16},{8,24},{16,0},{24,8},{1,17},{9,25},{17,1},{25,9},{2,18},{10... | collective-permute-start | bytes 393224 | tf_op jit(solution)/shard_map/ppermute | solution.py:34
  93.6 0.6 copy-start.6
  93.6 0.7 copy-start.7
  93.7 0.7 copy-start.8
  96.3 14.3 %collective-permute-start.11 = (f32[128,384]{1,0:T(8,128)}, f32[128,384]{1,0:T(8,128)S(1)}, u32[]{:S(2)}, u32[]{:S(2)}) collective-permute-start(f32[128,384]{1,0:T(8,128)} %shard_map.68), channel_id=1, source_target_pairs={{0,8},{8,16},{16,24},{24,0},{1,9},{9,17},{17,25},{25,1},{2,10},{10... | collective-permute-start | bytes 589832 | tf_op jit(solution)/shard_map/ppermute | solution.py:34
  96.5 45.0 %collective-permute-start.12 = (f32[128,384]{1,0:T(8,128)}, f32[128,384]{1,0:T(8,128)S(1)}, u32[]{:S(2)}, u32[]{:S(2)}) collective-permute-start(f32[128,384]{1,0:T(8,128)} %shard_map.68), channel_id=1, source_target_pairs={{0,16},{8,24},{16,0},{24,8},{1,17},{9,25},{17,1},{25,9},{2,18},{10... | collective-permute-start | bytes 589832 | tf_op jit(solution)/shard_map/ppermute | solution.py:34
  98.5 43.0 %collective-permute-start.13 = (f32[128,384]{1,0:T(8,128)}, f32[128,384]{1,0:T(8,128)S(1)}, u32[]{:S(2)}, u32[]{:S(2)}) collective-permute-start(f32[128,384]{1,0:T(8,128)} %shard_map.68), channel_id=1, source_target_pairs={{0,24},{8,0},{16,8},{24,16},{1,25},{9,1},{17,9},{25,17},{2,26},{10... | collective-permute-start | bytes 589832 | tf_op jit(solution)/shard_map/ppermute | solution.py:34
  142.5 20.5 %collective-permute-start.14 = (f32[512,384]{1,0:T(8,128)S(1)}, f32[512,384]{1,0:T(8,128)S(1)}, u32[]{:S(2)}, u32[]{:S(2)}) collective-permute-start(f32[512,384]{1,0:T(8,128)S(1)} %pad_maximum_fusion), channel_id=1, source_target_pairs={{0,1},{1,2},{2,3},{3,0},{4,5},{5,6},{6,7},{7,4},{8,9},{9,10},{10,1... | collective-permute-start | bytes 2359304 | tf_op jit(solution)/shard_map/ppermute | solution.py:34
  143.7 37.3 %collective-permute-start.15 = (f32[512,384]{1,0:T(8,128)S(1)}, f32[512,384]{1,0:T(8,128)S(1)}, u32[]{:S(2)}, u32[]{:S(2)}) collective-permute-start(f32[512,384]{1,0:T(8,128)S(1)} %pad_maximum_fusion), channel_id=1, source_target_pairs={{0,2},{1,3},{2,0},{3,1},{4,6},{5,7},{6,4},{7,5},{8,10},{9,11},{10,... | collective-permute-start | bytes 2359304 | tf_op jit(solution)/shard_map/ppermute | solution.py:34
  144.6 37.4 %collective-permute-start.16 = (f32[512,384]{1,0:T(8,128)S(1)}, f32[512,384]{1,0:T(8,128)S(1)}, u32[]{:S(2)}, u32[]{:S(2)}) collective-permute-start(f32[512,384]{1,0:T(8,128)S(1)} %pad_maximum_fusion), channel_id=1, source_target_pairs={{0,3},{1,0},{2,1},{3,2},{4,7},{5,4},{6,5},{7,6},{8,11},{9,8},{10,9... | collective-permute-start | bytes 2359304 | tf_op jit(solution)/shard_map/ppermute | solution.py:34
  145.7 131.7 %collective-permute-start.6 = (bf16[4608,512]{1,0:T(8,128)(2,1)}, bf16[4608,512]{1,0:T(8,128)(2,1)}, u32[]{:S(2)}, u32[]{:S(2)}) collective-permute-start(bf16[4608,512]{1,0:T(8,128)(2,1)} %constant_dynamic-update-slice_fusion.2.refs_9_.refs_2_.refs_3_), channel_id=1, source_target_pairs={{0,1},{1,0},{2,3},{3,2},{4,5},{5,4},{6,7},{7,6},{8,9},{9,8},{10,11... | collective-permute-start | bytes 14155784 | tf_op jit(solution)/shard_map/ppermute | solution.py:34
  147.3 131.3 %collective-permute-start.5 = (bf16[4608,512]{1,0:T(8,128)(2,1)}, bf16[4608,512]{1,0:T(8,128)(2,1)}, u32[]{:S(2)}, u32[]{:S(2)}) collective-permute-start(bf16[4608,512]{1,0:T(8,128)(2,1)} %constant_dynamic-update-slice_fusion.refs_8_.refs_0_.refs_1_), channel_id=1, source_target_pairs={{0,2},{2,0},{1,3},{3,1},{4,6},{6,4},{5,7},{7,5},{8,10},{10,8},{9,1... | collective-permute-start | bytes 14155784 | tf_op jit(solution)/shard_map/ppermute | solution.py:34
  182.9 6.0 %collective-permute-start.17 = (f32[2048,384]{1,0:T(8,128)}, f32[2048,384]{1,0:T(8,128)}, u32[]{:S(2)}, u32[]{:S(2)}) collective-permute-start(f32[2048,384]{1,0:T(8,128)} %constant_dynamic-update-slice_fusion.4.refs_0_), channel_id=1, source_target_pairs={{0,4},{4,0},{1,5},{5,1},{2,6},{6,2},{3,7},{7,3},{8,12},{12,8},{9,1... | collective-permute-start | bytes 9437192 | tf_op jit(solution)/shard_map/ppermute | solution.py:34
  422.9 20.9 %copy-start.1 = (f32[256,2304]{1,0:T(8,128)S(1)}, f32[256,2304]{1,0:T(8,128)}, u32[]{:S(2)}) copy-start(f32[256,2304]{1,0:T(8,128)} %param.7) | copy-start | bytes 7077892
Sparse Core Ops, SparseCore 0:
  11.3 246.0 all-gather.7
  259.0 80.4 all-gather.5
  341.1 46.0 all-gather.3

commit v2 on v1

--- a/solution.py
+++ b/solution.py
@@ -55,25 +55,28 @@
 
 
 def gather_tokens(halves, sizes, index):
-    near, far, near_starts, far_starts = [], [], [], []
+    rounds, starts = ([], [], []), ([], [], [])
     half = halves[0].shape[1]
     for part, start in enumerate(halves):
         order = (1, 0) if part == 0 else (0, 1)
         first, second = (COL[axis] for axis in order)
         size_first, size_second = (sizes[axis] for axis in order)
 
-        def token(by_first, by_second):
+        def add(place, piece, by_first, by_second):
             by = (by_second, by_first) if part == 0 else (by_first, by_second)
             at = [lax.rem(index[n] - by[n] + sizes[n], sizes[n]) for n in range(2)]
-            return ((at[0] * sizes[1] + at[1]) * 2 + part) * half
-
-        line = gathered_parts(start, first, size_first)
-        near.append(line)
-        near_starts += [token(by, 0) for by in range(size_first)]
+            rounds[place].append(piece)
+            starts[place].append(((at[0] * sizes[1] + at[1]) * 2 + part) * half)
+
+        add(0, start, 0, 0)
+        line = [start] + [shifted(start, first, size_first, by) for by in range(1, size_first)]
+        for by in range(1, size_first):
+            add(0, line[by], by, 0)
         for by_second in range(1, size_second):
-            far.append(shifted(line, second, size_second, by_second))
-            far_starts += [token(by, by_second) for by in range(size_first)]
-    return near, far, near_starts + far_starts
+            for by in range(size_first):
+                piece = shifted(line[by], second, size_second, by_second)
+                add(1 if by == 0 else 2, piece, by, by_second)
+    return rounds, sum(starts, [])
 
 
 def scattered(parts, axes, size, index):
@@ -87,6 +90,23 @@
 
 def gathered_parts(own, axes, size):
     return jnp.concatenate([own] + [shifted(own, axes, size, by) for by in range(1, size)], axis=0)
+
+
+def below(terms, after):
+    rows, columns = terms[0].shape
+
+    def kernel(*refs):
+        for k in range(len(terms)):
+            refs[-1][k * rows : (k + 1) * rows, :] = refs[k][...]
+
+    whole = pl.BlockSpec(memory_space=pltpu.VMEM)
+    return pl.pallas_call(
+        kernel,
+        in_specs=[whole] * len(terms) + [pl.BlockSpec(memory_space=pl.ANY)] * len(after),
+        out_specs=whole,
+        out_shape=jax.ShapeDtypeStruct((len(terms) * rows, columns), terms[0].dtype),
+        compiler_params=pltpu.CompilerParams(vmem_limit_bytes=VMEM_BYTES),
+    )(*terms, *after)
 
 
 def combine(left_terms, right_terms, after):
@@ -116,7 +136,7 @@
     )(*terms, *after)
 
 
-def finish(stacks, range_starts, test_starts, rank, after):
+def finish(stacks, range_starts, test_starts, rank):
     rank_z = stacks[0].shape[1] - rank
     blocks = range_starts.shape[0] // len(stacks)
     tokens = stacks[0].shape[0] * len(stacks)
@@ -157,7 +177,7 @@
         grid_spec=pltpu.PrefetchScalarGridSpec(
             num_scalar_prefetch=2,
             grid=(),
-            in_specs=[whole] * len(stacks) + [pl.BlockSpec(memory_space=pl.ANY)] * len(after),
+            in_specs=[whole] * len(stacks),
             out_specs=[whole] * 4,
             scratch_shapes=[
                 pltpu.VMEM((tokens, rank), jnp.float32),
@@ -171,7 +191,7 @@
             jax.ShapeDtypeStruct((rank_z, rank), jnp.float32),
         ],
         compiler_params=pltpu.CompilerParams(vmem_limit_bytes=VMEM_BYTES),
-    )(range_starts, test_starts, *stacks, *after)
+    )(range_starts, test_starts, *stacks)
 
 
 def assemble(stacks, starts, test_parts):
@@ -323,12 +343,12 @@
         unit = inputs.shape[0] // size_row
         range_terms = scattered(grads_range.reshape(size_col, unit, rank), COL, size_col, col)
         halves = turn(inputs, range_terms)
-        near, far, starts = gather_tokens(halves, (size_a, size_b), (a, b))
+        rounds, starts = gather_tokens(halves, (size_a, size_b), (a, b))
         test_inputs = test_inputs.reshape(size_z, size_core, unit, rank_z).transpose(1, 0, 2, 3)
         test_inputs = sum(scattered(test_inputs, "core", size_core, core))
         test_terms = scattered(test_inputs, "z", size_z, z)
-        own = combine(range_terms, test_terms, near)
-        own = gathered_parts(own, "z", size_z)
+        own = combine(range_terms, test_terms, rounds[0])
+        own = below([own] + [shifted(own, "z", size_z, by) for by in range(1, size_z)], rounds[1])
         own = gathered_parts(own, COL, size_col)
         stacks = [own] + [shifted(own, "core", size_core, by) for by in range(1, size_core)]
         at_core = lax.rem(core - jnp.arange(size_core) + size_core, size_core)[:, None, None]
@@ -342,14 +362,13 @@
             range_starts.reshape(-1).astype(jnp.int32),
             test_starts.reshape(-1).astype(jnp.int32),
             rank,
-            [],
         )
 
         gram_matrix = exact_product(core_input, core_input, ((0,), (0,)))
         factor_low = jnp.linalg.cholesky(gram_matrix)
         core_map = jax.scipy.linalg.cho_solve((factor_low, True), core_input.T)
 
-        rows_all, new_range, sketch_split = assemble(near + far, starts, range_parts)
+        rows_all, new_range, sketch_split = assemble(sum(rounds, []), starts, range_parts)
 
         out = ()
         for first, block, grads in gathered:

time: 457 us -> 425 us (0.930)
  the two profiles are of different devices: /device:TPU:26 before, /device:TPU:0 now
where the time goes in v2:
time: 425 us; the launch traced here: 419 us
  Pallas kernels  186 us (44%)
  waiting for transfers between devices  128 us (30%)
  starting transfers between devices  33.3 us (8%)
  other arithmetic  26.2 us (6%)
  matrix products  15.9 us (4%)
  local copies, waits for them, and re-layouts  14.6 us (3%)
  between operations  14.4 us (3%)
    pallas_call x3, Pallas kernels, slab(): pl.pallas_call(kernel, grid=(width // block, rows // tile), in_specs=in_s...  148 us
    ppermute x20, waiting for transfers between devices, shifted(): lax.ppermute(array, axes, [(i, (i + by) % size) for i in range(size)])  120 us
    ppermute x20, starting transfers between devices, shifted(): lax.ppermute(array, axes, [(i, (i + by) % size) for i in range(size)])  33.2 us
    pallas_call x1, Pallas kernels, assemble(): pl.pallas_call(kernel, grid_spec=pltpu.PrefetchScalarGridSpec(num_scalar_...  16.6 us
    dot_general x3, matrix products, exact_product(): lax.dot_general(left, right, (dims, ((), ())), precision=highest, preferr...  13.8 us
    another operation x3, other arithmetic, per_device(): factor_low = jnp.linalg.cholesky(gram_matrix)  12.4 us
    pallas_call x1, Pallas kernels, finish(): pl.pallas_call(kernel, grid_spec=pltpu.PrefetchScalarGridSpec(num_scalar_...  10.8 us
    another operation x2, other arithmetic, per_device(): core_map = jax.scipy.linalg.cho_solve((factor_low, True), core_input.T)  10.5 us
  transfers between devices with their start and end apart: 23, of which 14 were waited for; matrix products, arithmetic and copies ran while one was open for 12% of the time, Pallas kernels for 39%

profile of v2, /device:TPU:0, one launch (start us, length us, event | category | flops | bytes accessed | tf_op | source)
XLA Modules:
  0.0 418.8 jit_solution(1144676800951667208)
XLA Ops:
  7.2 3.9 slice.29
  11.2 2.3 slice.28
  13.6 6.5 %fusion.10 = f32[512,128]{1,0:T(8,128)S(1)} fusion(bf16[512,4608]{1,0:T(8,128)(2,1)} %param.5, f32[4608,128]{1,0:T(8,128)} %param.6), kind=kOutput, calls=%fused_computation.38 | convolution fusion | flops 3623878656 | bytes 7340032 | tf_op jit(solution)/shard_map/dot_general | solution.py:17
  20.8 2.9 collective-permute-start
  23.7 1.5 collective-permute-start.1
  25.2 1.4 collective-permute-start.2
  27.0 1.2 collective-permute-done.1.refs_2_
  28.2 1.3 collective-permute-done.2.refs_3_
  30.1 6.3 %shard_map.67 = (bf16[2304,512]{1,0:T(8,128)(2,1)}, bf16[2304,512]{1,0:T(8,128)(2,1)}) custom-call(bf16[1024,2304]{1,0:T(8,128)(2,1)} %array_ref.1, f32[128,128]{1,0:T(8,128)} %get-tuple-element.40.refs_0_, f32[128,128]{1,0:T(8,128)} %copy-done.3, f32[128,128]{1,0:T(8,128)} %copy-done.4, f32[128,128]{1,0:T(8,128)} %copy-done.5), custom_call_target="tpu_custom_call" | custom-call | tf_op jit(solution)/shard_map/pallas_call | solution.py:46
  36.4 1.2 collective-permute-start.3
  37.6 1.7 collective-permute-start.4
  39.6 0.9 collective-permute-start.6
  40.5 5.9 %fusion.11 = f32[1024,256]{1,0:T(8,128)S(1)} fusion(bf16[1024,2304]{1,0:T(8,128)(2,1)} %array_ref.1, f32[256,2304]{1,0:T(8,128)S(1)} %copy-done), kind=kOutput, calls=%fused_computation.39 | convolution fusion | flops 7247757312 | bytes 8126464 | tf_op jit(solution)/shard_map/dot_general | solution.py:17
  46.6 2.2 collective-permute-done.9
  48.8 0.7 dynamic-slice_bitcast_fusion.1
  49.5 1.3 collective-permute-start.10
  50.8 9.4 %collective-permute-done.10.refs_5_ = f32[128,256]{1,0:T(8,128)S(1)} collective-permute-done((f32[128,256]{1,0:T(8,128)S(1)}, f32[128,256]{1,0:T(8,128)S(1)}, u32[]{:S(2)}, u32[]{:S(2)}) %collective-permute-start.10) | collective-permute-done | bytes 131104 | tf_op jit(solution)/shard_map/ppermute | solution.py:34
  60.2 7.0 %collective-permute-start.11 = (f32[128,256]{1,0:T(8,128)S(1)}, f32[128,256]{1,0:T(8,128)S(1)}, u32[]{:S(2)}, u32[]{:S(2)}) collective-permute-start(f32[128,256]{1,0:T(8,128)S(1)} %get-tuple-element.34), channel_id=1, source_target_pairs={{0,16},{8,24},{16,0},{24,8},{1,17},{9,25},{17,1},{25,9},{2,18},{10... | collective-permute-start | bytes 393224 | tf_op jit(solution)/shard_map/ppermute | solution.py:34
  67.2 15.5 %collective-permute-done.11.refs_6_ = f32[128,256]{1,0:T(8,128)S(1)} collective-permute-done((f32[128,256]{1,0:T(8,128)S(1)}, f32[128,256]{1,0:T(8,128)S(1)}, u32[]{:S(2)}, u32[]{:S(2)}) %collective-permute-start.11) | collective-permute-done | bytes 131104 | tf_op jit(solution)/shard_map/ppermute | solution.py:34
  83.0 9.8 %collective-permute-done.12.refs_7_ = f32[128,256]{1,0:T(8,128)S(1)} collective-permute-done((f32[128,256]{1,0:T(8,128)S(1)}, f32[128,256]{1,0:T(8,128)S(1)}, u32[]{:S(2)}, u32[]{:S(2)}) %collective-permute-start.12) | collective-permute-done | bytes 131104 | tf_op jit(solution)/shard_map/ppermute | solution.py:34
  93.5 1.9 shard_map.68.refs_0_
  95.4 5.4 %collective-permute-start.13 = (f32[128,384]{1,0:T(8,128)}, f32[128,384]{1,0:T(8,128)S(1)}, u32[]{:S(2)}, u32[]{:S(2)}) collective-permute-start(f32[128,384]{1,0:T(8,128)} %shard_map.68.refs_0_), channel_id=1, source_target_pairs={{0,8},{8,16},{16,24},{24,0},{1,9},{9,17},{17,25},{25,1},{2,10},{10... | collective-permute-start | bytes 589832 | tf_op jit(solution)/shard_map/ppermute | solution.py:34
  100.8 2.4 collective-permute-start.15
  103.1 37.2 %collective-permute-done.5.refs_4_ = bf16[2304,512]{1,0:T(8,128)(2,1)} collective-permute-done((bf16[2304,512]{1,0:T(8,128)(2,1)}, bf16[2304,512]{1,0:T(8,128)(2,1)}, u32[]{:S(2)}, u32[]{:S(2)}) %collective-permute-start.5) | collective-permute-done | bytes 2359328 | tf_op jit(solution)/shard_map/ppermute | solution.py:34
  141.8 2.1 shard_map.69
  143.9 0.8 collective-permute-start.16
  144.7 0.9 collective-permute-start.17
  145.6 2.3 collective-permute-start.18
  148.0 17.6 %collective-permute-done.16 = f32[512,384]{1,0:T(8,128)S(1)} collective-permute-done((f32[512,384]{1,0:T(8,128)}, f32[512,384]{1,0:T(8,128)S(1)}, u32[]{:S(2)}, u32[]{:S(2)}) %collective-permute-start.16) | collective-permute-done | bytes 786464 | tf_op jit(solution)/shard_map/ppermute | solution.py:34
  165.5 13.1 %collective-permute-done.17 = f32[512,384]{1,0:T(8,128)S(1)} collective-permute-done((f32[512,384]{1,0:T(8,128)}, f32[512,384]{1,0:T(8,128)S(1)}, u32[]{:S(2)}, u32[]{:S(2)}) %collective-permute-start.17) | collective-permute-done | bytes 786464 | tf_op jit(solution)/shard_map/ppermute | solution.py:34
  178.6 3.0 pad_maximum_fusion.refs_0_
  181.7 1.9 slice.27
  183.6 1.1 collective-permute-start.7
  184.7 1.7 collective-permute-start.8
  188.5 10.8 %shard_map.70 = (bf16[4096,256]{1,0:T(8,128)(2,1)}, bf16[256,4096]{1,0:T(8,128)(2,1)}, bf16[256,4096]{1,0:T(8,128)(2,1)}, f32[256,128]{1,0:T(8,128)}) custom-call(s32[32]{0:T(128)} %mul.111.range_starts_ref, s32[32]{0:T(128)} %mul.114.test_starts_ref, f32[2048,384]{1,0:T(8,128)} %pad_maximum_fusion.refs_0_, f32[2048,384]{1,0:T(8,128)} %collective-permute-done.19.refs_1_), custom_call_target="tpu_custom_call" | custom-call | tf_op jit(solution)/shard_map/pallas_call | solution.py:175
  199.3 1.4 fusion.12
  200.8 11.7 %cholesky.16 = f32[128,128]{1,0:T(8,128)S(1)} custom-call(f32[128,128]{1,0:T(8,128)S(1)} %fusion.5), custom_call_target="Cholesky" | custom-call | tf_op jit(solution)/shard_map/jit(cholesky)/cholesky | solution.py:368
  213.9 9.8 %custom-call.10 = f32[1,128,128]{1,2,0:T(8,128)S(1)} custom-call(f32[1,128,128]{2,1,0:T(8,128)S(1)} %fusion), custom_call_target="InvertDiagBlocksLowerTriangular" | custom-call | tf_op jit(solution)/shard_map/jit(_cho_solve)/triangular_solve | solution.py:369
  223.7 1.2 fusion.3
  224.9 0.9 fusion.1.map_ref
  225.8 11.7 %collective-permute-done.7.refs_6_ = bf16[2304,512]{1,0:T(8,128)(2,1)S(1)} collective-permute-done((bf16[2304,512]{1,0:T(8,128)(2,1)}, bf16[2304,512]{1,0:T(8,128)(2,1)S(1)}, u32[]{:S(2)}, u32[]{:S(2)}) %collective-permute-start.7) | collective-permute-done | bytes 2359328 | tf_op jit(solution)/shard_map/ppermute | solution.py:34
  237.5 0.9 collective-permute-done.8.refs_7_
  238.9 16.6 %shard_map.71 = (bf16[2304,4096]{1,0:T(8,128)(2,1)}, f32[2304,128]{1,0:T(8,128)}, bf16[2304,384]{1,0:T(8,128)(2,1)}) custom-call(s32[8]{0:T(128)} %stack.35.starts_ref, bf16[2304,512]{1,0:T(8,128)(2,1)} %get-tuple-element.18.refs_8_.refs_0_, bf16[2304,512]{1,0:T(8,128)(2,1)} %collective-permute-done.3.refs_9_.refs_1_, ...), custom_call_target="tpu_custom_call" | custom-call | flops 4831838208 | bytes 37748736 | tf_op jit(solution)/shard_map/pallas_call | solution.py:224
  255.5 6.2 %all-gather.8.cloned.1.call-done.grads_ref = bf16[4096,3072]{1,0:T(8,128)(2,1)} async-done(((bf16[512,3072]{1,0:T(8,128)(2,1)}), bf16[4096,3072]{1,0:T(8,128)(2,1)}) %all-gather.8.cloned.1.call-update) | async-done | bytes 25165840 | tf_op jit(solution)/shard_map/all_gather | solution.py:338
  261.8 91.4 %shard_map.72 = (f32[256,4608]{1,0:T(8,128)}, f32[2304,4608]{1,0:T(8,128)}) custom-call(bf16[2304,4096]{1,0:T(8,128)(2,1)} %get-tuple-element.22.rows_ref, bf16[4096,3072]{1,0:T(8,128)(2,1)} %all-gather.8.cloned.1.call-done.grads_ref, bf16[2304,384]{1,0:T(8,128)(2,1)} %get-tuple-element.23.split_ref, bf16[256,4096]{1,0:T(8,128)(2,1)} %get-tuple-element.24.high_ref, ...), custom_call_target="tpu_custom_call" | custom-call | flops 76302778368 | bytes 72351744 | tf_op jit(solution)/shard_map/pallas_call | solution.py:283
  353.2 36.1 %shard_map.73 = (f32[256,4608]{1,0:T(8,128)}, f32[2304,4608]{1,0:T(8,128)}) custom-call(bf16[2304,4096]{1,0:T(8,128)(2,1)} %get-tuple-element.22.rows_ref, bf16[4096,1024]{1,0:T(8,128)(2,1)} %all-gather.6.cloned.1.call-done.grads_ref, bf16[2304,384]{1,0:T(8,128)(2,1)} %get-tuple-element.23.split_ref, ...), custom_call_target="tpu_custom_call", output_to_operand_aliasing={{0}: (6, {}), {1}: (7, {})} | custom-call | flops 25434259456 | bytes 36700160 | tf_op jit(solution)/shard_map/pallas_call | solution.py:283
  389.3 1.7 all-gather.4.cloned.1.call-done.grads_ref
  391.0 20.9 %shard_map.74 = (f32[256,4608]{1,0:T(8,128)}, f32[2304,4608]{1,0:T(8,128)}) custom-call(bf16[2304,4096]{1,0:T(8,128)(2,1)} %get-tuple-element.22.rows_ref, bf16[4096,512]{1,0:T(8,128)(2,1)} %all-gather.4.cloned.1.call-done.grads_ref, bf16[2304,384]{1,0:T(8,128)(2,1)} %get-tuple-element.23.split_ref, ...), custom_call_target="tpu_custom_call", output_to_operand_aliasing={{0}: (6, {}), {1}: (7, {})} | custom-call | flops 12717129728 | bytes 27787264 | tf_op jit(solution)/shard_map/pallas_call | solution.py:283
  (62 shorter events, 8.6 us)
Async XLA Ops:
  7.2 33.3 %copy-start = (f32[256,2304]{1,0:T(8,128)S(1)}, f32[256,2304]{1,0:T(8,128)}, u32[]{:S(2)}) copy-start(f32[256,2304]{1,0:T(8,128)} %param.7) | copy-start | bytes 7077892
  7.2 254.6 %all-gather.8.cloned.1.call-start = ((), (), s32[]{:S(2)}) async-start(), calls=%async_computation.2 | async-start | bytes 28311552 | tf_op jit(solution)/shard_map/all_gather | solution.py:338
  11.2 342.0 %all-gather.6.cloned.1.call-start = ((), (), s32[]{:S(2)}) async-start(), calls=%async_computation.1 | async-start | bytes 9437184 | tf_op jit(solution)/shard_map/all_gather | solution.py:338
  13.5 377.5 %all-gather.4.cloned.1.call-start = ((), (), s32[]{:S(2)}) async-start(), calls=%async_computation | async-start | bytes 4718592 | tf_op jit(solution)/shard_map/all_gather | solution.py:338
  20.8 6.2 %collective-permute-start = (f32[128,128]{1,0:T(8,128)S(1)}, f32[128,128]{1,0:T(8,128)S(1)}, u32[]{:S(2)}, u32[]{:S(2)}) collective-permute-start(f32[128,128]{1,0:T(8,128)S(1)} %get-tuple-element.39), channel_id=1, source_target_pairs={{0,1},{1,2},{2,3},{3,0},{4,5},{5,6},{6,7},{7,4},{8,9},{9,10},{10,1... | collective-permute-start | bytes 196616 | tf_op jit(solution)/shard_map/ppermute | solution.py:34
  23.7 4.4 %collective-permute-start.1 = (f32[128,128]{1,0:T(8,128)S(1)}, f32[128,128]{1,0:T(8,128)S(1)}, u32[]{:S(2)}, u32[]{:S(2)}) collective-permute-start(f32[128,128]{1,0:T(8,128)S(1)} %get-tuple-element.38), channel_id=1, source_target_pairs={{0,2},{1,3},{2,0},{3,1},{4,6},{5,7},{6,4},{7,5},{8,10},{9,11},{10,... | collective-permute-start | bytes 196616 | tf_op jit(solution)/shard_map/ppermute | solution.py:34
  25.2 4.3 %collective-permute-start.2 = (f32[128,128]{1,0:T(8,128)S(1)}, f32[128,128]{1,0:T(8,128)S(1)}, u32[]{:S(2)}, u32[]{:S(2)}) collective-permute-start(f32[128,128]{1,0:T(8,128)S(1)} %get-tuple-element.37), channel_id=1, source_target_pairs={{0,3},{1,0},{2,1},{3,2},{4,7},{5,4},{6,5},{7,6},{8,11},{9,8},{10,9... | collective-permute-start | bytes 196616 | tf_op jit(solution)/shard_map/ppermute | solution.py:34
  27.0 2.5 copy-start.3
  28.2 1.3 copy-start.4
  29.5 0.6 copy-start.5
  36.4 56.4 %collective-permute-start.3 = (bf16[2304,512]{1,0:T(8,128)(2,1)}, bf16[2304,512]{1,0:T(8,128)(2,1)}, u32[]{:S(2)}, u32[]{:S(2)}) collective-permute-start(bf16[2304,512]{1,0:T(8,128)(2,1)} %get-tuple-element.18.refs_8_.refs_0_), channel_id=1, source_target_pairs={{0,1},{1,0},{2,3},{3,2},{4,5},{5,4},{6,7},{7,6},{8,9},{9,8},{10,11... | collective-permute-start | bytes 7077896 | tf_op jit(solution)/shard_map/ppermute | solution.py:34
  37.6 55.2 %collective-permute-start.4 = (bf16[2304,512]{1,0:T(8,128)(2,1)}, bf16[2304,512]{1,0:T(8,128)(2,1)}, u32[]{:S(2)}, u32[]{:S(2)}) collective-permute-start(bf16[2304,512]{1,0:T(8,128)(2,1)} %get-tuple-element.19.refs_10_.refs_2_), channel_id=1, source_target_pairs={{0,2},{2,0},{1,3},{3,1},{4,6},{6,4},{5,7},{7,5},{8,10},{10,8},{9,1... | collective-permute-start | bytes 7077896 | tf_op jit(solution)/shard_map/ppermute | solution.py:34
  39.4 101.0 %collective-permute-start.5 = (bf16[2304,512]{1,0:T(8,128)(2,1)}, bf16[2304,512]{1,0:T(8,128)(2,1)}, u32[]{:S(2)}, u32[]{:S(2)}) collective-permute-start(bf16[2304,512]{1,0:T(8,128)(2,1)} %get-tuple-element.18.refs_8_.refs_0_), channel_id=1, source_target_pairs={{0,2},{2,0},{1,3},{3,1},{4,6},{6,4},{5,7},{7,5},{8,10},{10,8},{9,1... | collective-permute-start | bytes 7077896 | tf_op jit(solution)/shard_map/ppermute | solution.py:34
  39.6 100.7 %collective-permute-start.6 = (bf16[2304,512]{1,0:T(8,128)(2,1)}, bf16[2304,512]{1,0:T(8,128)(2,1)}, u32[]{:S(2)}, u32[]{:S(2)}) collective-permute-start(bf16[2304,512]{1,0:T(8,128)(2,1)} %get-tuple-element.19.refs_10_.refs_2_), channel_id=1, source_target_pairs={{0,1},{1,0},{2,3},{3,2},{4,5},{5,4},{6,7},{7,6},{8,9},{9,8},{10,11... | collective-permute-start | bytes 7077896 | tf_op jit(solution)/shard_map/ppermute | solution.py:34
  46.5 2.3 collective-permute-start.9
  49.5 10.7 %collective-permute-start.10 = (f32[128,256]{1,0:T(8,128)S(1)}, f32[128,256]{1,0:T(8,128)S(1)}, u32[]{:S(2)}, u32[]{:S(2)}) collective-permute-start(f32[128,256]{1,0:T(8,128)S(1)} %get-tuple-element.35), channel_id=1, source_target_pairs={{0,8},{8,16},{16,24},{24,0},{1,9},{9,17},{17,25},{25,1},{2,10},{10... | collective-permute-start | bytes 393224 | tf_op jit(solution)/shard_map/ppermute | solution.py:34
  60.2 32.6 %copy-start.9 = (f32[128,256]{1,0:T(8,128)}, f32[128,256]{1,0:T(8,128)S(1)}, u32[]{:S(2)}) copy-start(f32[128,256]{1,0:T(8,128)S(1)} %collective-permute-done.10.refs_5_) | copy-start | bytes 393220
  60.2 22.6 %collective-permute-start.11 = (f32[128,256]{1,0:T(8,128)S(1)}, f32[128,256]{1,0:T(8,128)S(1)}, u32[]{:S(2)}, u32[]{:S(2)}) collective-permute-start(f32[128,256]{1,0:T(8,128)S(1)} %get-tuple-element.34), channel_id=1, source_target_pairs={{0,16},{8,24},{16,0},{24,8},{1,17},{9,25},{17,1},{25,9},{2,18},{10... | collective-permute-start | bytes 393224 | tf_op jit(solution)/shard_map/ppermute | solution.py:34
  82.8 10.0 %copy-start.10 = (f32[128,256]{1,0:T(8,128)}, f32[128,256]{1,0:T(8,128)S(1)}, u32[]{:S(2)}) copy-start(f32[128,256]{1,0:T(8,128)S(1)} %collective-permute-done.11.refs_6_) | copy-start | bytes 393220
  82.8 10.0 %collective-permute-start.12 = (f32[128,256]{1,0:T(8,128)S(1)}, f32[128,256]{1,0:T(8,128)S(1)}, u32[]{:S(2)}, u32[]{:S(2)}) collective-permute-start(f32[128,256]{1,0:T(8,128)S(1)} %get-tuple-element.33), channel_id=1, source_target_pairs={{0,24},{8,0},{16,8},{24,16},{1,25},{9,1},{17,9},{25,17},{2,26},{10... | collective-permute-start | bytes 393224 | tf_op jit(solution)/shard_map/ppermute | solution.py:34
  92.8 0.6 copy-start.11
  95.4 45.0 %collective-permute-start.13 = (f32[128,384]{1,0:T(8,128)}, f32[128,384]{1,0:T(8,128)S(1)}, u32[]{:S(2)}, u32[]{:S(2)}) collective-permute-start(f32[128,384]{1,0:T(8,128)} %shard_map.68.refs_0_), channel_id=1, source_target_pairs={{0,8},{8,16},{16,24},{24,0},{1,9},{9,17},{17,25},{25,1},{2,10},{10... | collective-permute-start | bytes 589832 | tf_op jit(solution)/shard_map/ppermute | solution.py:34
  100.8 39.6 %collective-permute-start.14 = (f32[128,384]{1,0:T(8,128)}, f32[128,384]{1,0:T(8,128)S(1)}, u32[]{:S(2)}, u32[]{:S(2)}) collective-permute-start(f32[128,384]{1,0:T(8,128)} %shard_map.68.refs_0_), channel_id=1, source_target_pairs={{0,16},{8,24},{16,0},{24,8},{1,17},{9,25},{17,1},{25,9},{2,18},{10... | collective-permute-start | bytes 589832 | tf_op jit(solution)/shard_map/ppermute | solution.py:34
  100.8 39.6 %collective-permute-start.15 = (f32[128,384]{1,0:T(8,128)}, f32[128,384]{1,0:T(8,128)S(1)}, u32[]{:S(2)}, u32[]{:S(2)}) collective-permute-start(f32[128,384]{1,0:T(8,128)} %shard_map.68.refs_0_), channel_id=1, source_target_pairs={{0,24},{8,0},{16,8},{24,16},{1,25},{9,1},{17,9},{25,17},{2,26},{10... | collective-permute-start | bytes 589832 | tf_op jit(solution)/shard_map/ppermute | solution.py:34
  140.3 0.7 copy-start.6
  140.4 0.7 copy-start.7
  141.1 0.7 copy-start.8
  143.9 21.6 %collective-permute-start.16 = (f32[512,384]{1,0:T(8,128)}, f32[512,384]{1,0:T(8,128)S(1)}, u32[]{:S(2)}, u32[]{:S(2)}) collective-permute-start(f32[512,384]{1,0:T(8,128)} %shard_map.69), channel_id=1, source_target_pairs={{0,1},{1,2},{2,3},{3,0},{4,5},{5,6},{6,7},{7,4},{8,9},{9,10},{10,1... | collective-permute-start | bytes 2359304 | tf_op jit(solution)/shard_map/ppermute | solution.py:34
  144.7 33.9 %collective-permute-start.17 = (f32[512,384]{1,0:T(8,128)}, f32[512,384]{1,0:T(8,128)S(1)}, u32[]{:S(2)}, u32[]{:S(2)}) collective-permute-start(f32[512,384]{1,0:T(8,128)} %shard_map.69), channel_id=1, source_target_pairs={{0,2},{1,3},{2,0},{3,1},{4,6},{5,7},{6,4},{7,5},{8,10},{9,11},{10,... | collective-permute-start | bytes 2359304 | tf_op jit(solution)/shard_map/ppermute | solution.py:34
  145.6 33.0 %collective-permute-start.18 = (f32[512,384]{1,0:T(8,128)}, f32[512,384]{1,0:T(8,128)S(1)}, u32[]{:S(2)}, u32[]{:S(2)}) collective-permute-start(f32[512,384]{1,0:T(8,128)} %shard_map.69), channel_id=1, source_target_pairs={{0,3},{1,0},{2,1},{3,2},{4,7},{5,4},{6,5},{7,6},{8,11},{9,8},{10,9... | collective-permute-start | bytes 2359304 | tf_op jit(solution)/shard_map/ppermute | solution.py:34
  181.6 6.9 %collective-permute-start.19 = (f32[2048,384]{1,0:T(8,128)}, f32[2048,384]{1,0:T(8,128)}, u32[]{:S(2)}, u32[]{:S(2)}) collective-permute-start(f32[2048,384]{1,0:T(8,128)} %pad_maximum_fusion.refs_0_), channel_id=1, source_target_pairs={{0,4},{4,0},{1,5},{5,1},{2,6},{6,2},{3,7},{7,3},{8,12},{12,8},{9,1... | collective-permute-start | bytes 9437192 | tf_op jit(solution)/shard_map/ppermute | solution.py:34
  183.6 53.9 %collective-permute-start.7 = (bf16[2304,512]{1,0:T(8,128)(2,1)}, bf16[2304,512]{1,0:T(8,128)(2,1)S(1)}, u32[]{:S(2)}, u32[]{:S(2)}) collective-permute-start(bf16[2304,512]{1,0:T(8,128)(2,1)} %collective-permute-done.3.refs_9_.refs_1_), channel_id=1, source_target_pairs={{0,2},{2,0},{1,3},{3,1},{4,6},{6,4},{5,7},{7,5},{8,10},{10,8},{9,1... | collective-permute-start | bytes 7077896 | tf_op jit(solution)/shard_map/ppermute | solution.py:34
  184.7 53.7 %collective-permute-start.8 = (bf16[2304,512]{1,0:T(8,128)(2,1)}, bf16[2304,512]{1,0:T(8,128)(2,1)}, u32[]{:S(2)}, u32[]{:S(2)}) collective-permute-start(bf16[2304,512]{1,0:T(8,128)(2,1)} %collective-permute-done.4.refs_11_.refs_3_), channel_id=1, source_target_pairs={{0,1},{1,0},{2,3},{3,2},{4,5},{5,4},{6,7},{7,6},{8,9},{9,8},{10,11... | collective-permute-start | bytes 7077896 | tf_op jit(solution)/shard_map/ppermute | solution.py:34
  237.5 1.4 copy-start.2
  391.0 20.9 %copy-start.1 = (f32[256,2304]{1,0:T(8,128)S(1)}, f32[256,2304]{1,0:T(8,128)}, u32[]{:S(2)}) copy-start(f32[256,2304]{1,0:T(8,128)} %param.7) | copy-start | bytes 7077892
Sparse Core Ops, SparseCore 0:
  11.3 250.4 all-gather.7
  263.4 80.2 all-gather.5
  345.3 45.6 all-gather.3

commit v3 on v2

--- a/solution.py
+++ b/solution.py
@@ -250,10 +250,24 @@
     width = grads.shape[1]
     rank, rank_z = core_map.shape
     tile = largest_tile(rows, 768)
+    turns = rows // tile
     at = first // block
 
     def kernel(rows_ref, grads_ref, split_ref, high_ref, low_ref, map_ref, *refs):
-        corange_ref, residual_ref, project_ref = refs[-3:]
+        corange_ref, residual_ref, project_ref, tiles_ref, sems = refs[-5:]
+        step = pl.program_id(0) * turns + pl.program_id(1)
+        slot = lax.rem(step, 2)
+
+        def fetch(at_step):
+            tile_at = pl.multiple_of(lax.rem(at_step, turns) * tile, tile)
+            to = lax.rem(at_step, 2)
+            return pltpu.make_async_copy(
+                rows_ref.at[pl.ds(tile_at, tile), :], tiles_ref.at[to], sems.at[to]
+            )
+
+        @pl.when(step == 0)
+        def _():
+            fetch(step).start()
 
         @pl.when(pl.program_id(1) == 0)
         def _():
@@ -268,12 +282,18 @@
             project_ref[rank : 2 * rank, :] = high
             project_ref[2 * rank :, :] = low
 
+        fetch(step).wait()
+
+        @pl.when(step + 1 < turns * (width // block))
+        def _():
+            fetch(step + 1).start()
+
         residual_ref[...] = jnp.dot(
-            rows_ref[...], grads_ref[...], preferred_element_type=jnp.float32
+            tiles_ref[slot], grads_ref[...], preferred_element_type=jnp.float32
         ) + jnp.dot(split_ref[...], project_ref[...], preferred_element_type=jnp.float32)
 
     in_specs = [
-        pl.BlockSpec((tile, tokens), lambda j, i: (i, 0)),
+        pl.BlockSpec(memory_space=pl.ANY),
         pl.BlockSpec((tokens, block), lambda j, i: (0, j)),
         pl.BlockSpec((tile, 3 * rank), lambda j, i: (i, 0)),
         pl.BlockSpec((rank_z, tokens), lambda j, i: (0, 0)),
@@ -292,7 +312,11 @@
             jax.ShapeDtypeStruct((rank_z, columns), jnp.float32),
             jax.ShapeDtypeStruct((rows, columns), jnp.float32),
         ],
-        scratch_shapes=[pltpu.VMEM((3 * rank, block), jnp.bfloat16)],
+        scratch_shapes=[
+            pltpu.VMEM((3 * rank, block), jnp.bfloat16),
+            pltpu.VMEM((2, tile, tokens), jnp.bfloat16),
+            pltpu.SemaphoreType.DMA((2,)),
+        ],
         input_output_aliases={6: 0, 7: 1} if before else {},
         compiler_params=pltpu.CompilerParams(vmem_limit_bytes=VMEM_BYTES),
         cost_estimate=pl.CostEstimate(

time: 425 us -> 423 us (level)
  Pallas kernels: 186 us -> 181 us
    pallas_call x3, Pallas kernels: 148 us -> 143 us  [slab(): pl.pallas_call(kernel, grid=(width // block, rows // tile), in_specs=in_s...]
where the time goes in v3:
time: 423 us; the launch traced here: 417 us
  Pallas kernels  181 us (43%)
  waiting for transfers between devices  132 us (31%)
  starting transfers between devices  33.3 us (8%)
  other arithmetic  26.2 us (6%)
  matrix products  15.9 us (4%)
  local copies, waits for them, and re-layouts  14.6 us (3%)
  between operations  14.5 us (3%)
    pallas_call x3, Pallas kernels, slab(): pl.pallas_call(kernel, grid=(width // block, rows // tile), in_specs=in_s...  143 us
    ppermute x20, waiting for transfers between devices, shifted(): lax.ppermute(array, axes, [(i, (i + by) % size) for i in range(size)])  120 us
    ppermute x20, starting transfers between devices, shifted(): lax.ppermute(array, axes, [(i, (i + by) % size) for i in range(size)])  33.2 us
    pallas_call x1, Pallas kernels, assemble(): pl.pallas_call(kernel, grid_spec=pltpu.PrefetchScalarGridSpec(num_scalar_...  16.6 us
    dot_general x3, matrix products, exact_product(): lax.dot_general(left, right, (dims, ((), ())), precision=highest, preferr...  13.8 us
    another operation x3, other arithmetic, per_device(): factor_low = jnp.linalg.cholesky(gram_matrix)  12.4 us
    all_gather x3, waiting for transfers between devices, per_device(): lax.all_gather(part, ROW, axis=0, tiled=True)  11.4 us
    pallas_call x1, Pallas kernels, finish(): pl.pallas_call(kernel, grid_spec=pltpu.PrefetchScalarGridSpec(num_scalar_...  10.8 us
  transfers between devices with their start and end apart: 23, of which 14 were waited for; matrix products, arithmetic and copies ran while one was open for 12% of the time, Pallas kernels for 39%

profile of v3, /device:TPU:0, one launch (start us, length us, event | category | flops | bytes accessed | tf_op | source)
XLA Modules:
  0.0 417.2 jit_solution(1545276220925319062)
XLA Ops:
  7.2 3.9 slice.29
  11.2 2.3 slice.28
  13.6 6.5 %fusion.10 = f32[512,128]{1,0:T(8,128)S(1)} fusion(bf16[512,4608]{1,0:T(8,128)(2,1)} %param.5, f32[4608,128]{1,0:T(8,128)} %param.6), kind=kOutput, calls=%fused_computation.38 | convolution fusion | flops 3623878656 | bytes 7340032 | tf_op jit(solution)/shard_map/dot_general | solution.py:17
  20.8 2.9 collective-permute-start
  23.7 1.5 collective-permute-start.1
  25.2 1.4 collective-permute-start.2
  27.0 1.2 collective-permute-done.1.refs_2_
  28.2 1.3 collective-permute-done.2.refs_3_
  30.1 6.3 %shard_map.67 = (bf16[2304,512]{1,0:T(8,128)(2,1)}, bf16[2304,512]{1,0:T(8,128)(2,1)}) custom-call(bf16[1024,2304]{1,0:T(8,128)(2,1)} %array_ref.1, f32[128,128]{1,0:T(8,128)} %get-tuple-element.40.refs_0_, f32[128,128]{1,0:T(8,128)} %copy-done.3, f32[128,128]{1,0:T(8,128)} %copy-done.4, f32[128,128]{1,0:T(8,128)} %copy-done.5), custom_call_target="tpu_custom_call" | custom-call | tf_op jit(solution)/shard_map/pallas_call | solution.py:46
  36.4 1.2 collective-permute-start.3
  37.6 1.7 collective-permute-start.4
  39.6 0.9 collective-permute-start.6
  40.5 5.9 %fusion.11 = f32[1024,256]{1,0:T(8,128)S(1)} fusion(bf16[1024,2304]{1,0:T(8,128)(2,1)} %array_ref.1, f32[256,2304]{1,0:T(8,128)S(1)} %copy-done), kind=kOutput, calls=%fused_computation.39 | convolution fusion | flops 7247757312 | bytes 8126464 | tf_op jit(solution)/shard_map/dot_general | solution.py:17
  46.6 2.2 collective-permute-done.9
  48.8 0.7 dynamic-slice_bitcast_fusion.1
  49.5 1.3 collective-permute-start.10
  50.8 9.4 %collective-permute-done.10.refs_5_ = f32[128,256]{1,0:T(8,128)S(1)} collective-permute-done((f32[128,256]{1,0:T(8,128)S(1)}, f32[128,256]{1,0:T(8,128)S(1)}, u32[]{:S(2)}, u32[]{:S(2)}) %collective-permute-start.10) | collective-permute-done | bytes 131104 | tf_op jit(solution)/shard_map/ppermute | solution.py:34
  60.2 7.0 %collective-permute-start.11 = (f32[128,256]{1,0:T(8,128)S(1)}, f32[128,256]{1,0:T(8,128)S(1)}, u32[]{:S(2)}, u32[]{:S(2)}) collective-permute-start(f32[128,256]{1,0:T(8,128)S(1)} %get-tuple-element.34), channel_id=1, source_target_pairs={{0,16},{8,24},{16,0},{24,8},{1,17},{9,25},{17,1},{25,9},{2,18},{10... | collective-permute-start | bytes 393224 | tf_op jit(solution)/shard_map/ppermute | solution.py:34
  67.2 15.5 %collective-permute-done.11.refs_6_ = f32[128,256]{1,0:T(8,128)S(1)} collective-permute-done((f32[128,256]{1,0:T(8,128)S(1)}, f32[128,256]{1,0:T(8,128)S(1)}, u32[]{:S(2)}, u32[]{:S(2)}) %collective-permute-start.11) | collective-permute-done | bytes 131104 | tf_op jit(solution)/shard_map/ppermute | solution.py:34
  83.0 9.8 %collective-permute-done.12.refs_7_ = f32[128,256]{1,0:T(8,128)S(1)} collective-permute-done((f32[128,256]{1,0:T(8,128)S(1)}, f32[128,256]{1,0:T(8,128)S(1)}, u32[]{:S(2)}, u32[]{:S(2)}) %collective-permute-start.12) | collective-permute-done | bytes 131104 | tf_op jit(solution)/shard_map/ppermute | solution.py:34
  93.5 1.9 shard_map.68.refs_0_
  95.4 5.4 %collective-permute-start.13 = (f32[128,384]{1,0:T(8,128)}, f32[128,384]{1,0:T(8,128)S(1)}, u32[]{:S(2)}, u32[]{:S(2)}) collective-permute-start(f32[128,384]{1,0:T(8,128)} %shard_map.68.refs_0_), channel_id=1, source_target_pairs={{0,8},{8,16},{16,24},{24,0},{1,9},{9,17},{17,25},{25,1},{2,10},{10... | collective-permute-start | bytes 589832 | tf_op jit(solution)/shard_map/ppermute | solution.py:34
  100.8 2.4 collective-permute-start.15
  103.1 37.2 %collective-permute-done.5.refs_4_ = bf16[2304,512]{1,0:T(8,128)(2,1)} collective-permute-done((bf16[2304,512]{1,0:T(8,128)(2,1)}, bf16[2304,512]{1,0:T(8,128)(2,1)}, u32[]{:S(2)}, u32[]{:S(2)}) %collective-permute-start.5) | collective-permute-done | bytes 2359328 | tf_op jit(solution)/shard_map/ppermute | solution.py:34
  141.8 2.1 shard_map.69
  143.9 0.8 collective-permute-start.16
  144.7 0.9 collective-permute-start.17
  145.6 2.3 collective-permute-start.18
  148.0 17.6 %collective-permute-done.16 = f32[512,384]{1,0:T(8,128)S(1)} collective-permute-done((f32[512,384]{1,0:T(8,128)}, f32[512,384]{1,0:T(8,128)S(1)}, u32[]{:S(2)}, u32[]{:S(2)}) %collective-permute-start.16) | collective-permute-done | bytes 786464 | tf_op jit(solution)/shard_map/ppermute | solution.py:34
  165.5 13.1 %collective-permute-done.17 = f32[512,384]{1,0:T(8,128)S(1)} collective-permute-done((f32[512,384]{1,0:T(8,128)}, f32[512,384]{1,0:T(8,128)S(1)}, u32[]{:S(2)}, u32[]{:S(2)}) %collective-permute-start.17) | collective-permute-done | bytes 786464 | tf_op jit(solution)/shard_map/ppermute | solution.py:34
  178.6 3.0 pad_maximum_fusion.refs_0_
  181.7 1.9 slice.27
  183.6 1.1 collective-permute-start.7
  184.7 1.7 collective-permute-start.8
  188.5 10.8 %shard_map.70 = (bf16[4096,256]{1,0:T(8,128)(2,1)}, bf16[256,4096]{1,0:T(8,128)(2,1)}, bf16[256,4096]{1,0:T(8,128)(2,1)}, f32[256,128]{1,0:T(8,128)}) custom-call(s32[32]{0:T(128)} %mul.111.range_starts_ref, s32[32]{0:T(128)} %mul.114.test_starts_ref, f32[2048,384]{1,0:T(8,128)} %pad_maximum_fusion.refs_0_, f32[2048,384]{1,0:T(8,128)} %collective-permute-done.19.refs_1_), custom_call_target="tpu_custom_call" | custom-call | tf_op jit(solution)/shard_map/pallas_call | solution.py:175
  199.3 1.4 fusion.12
  200.8 11.7 %cholesky.16 = f32[128,128]{1,0:T(8,128)S(1)} custom-call(f32[128,128]{1,0:T(8,128)S(1)} %fusion.5), custom_call_target="Cholesky" | custom-call | tf_op jit(solution)/shard_map/jit(cholesky)/cholesky | solution.py:392
  213.9 9.8 %custom-call.10 = f32[1,128,128]{1,2,0:T(8,128)S(1)} custom-call(f32[1,128,128]{2,1,0:T(8,128)S(1)} %fusion), custom_call_target="InvertDiagBlocksLowerTriangular" | custom-call | tf_op jit(solution)/shard_map/jit(_cho_solve)/triangular_solve | solution.py:393
  223.7 1.2 fusion.3
  224.9 0.9 fusion.1.map_ref
  225.8 11.7 %collective-permute-done.7.refs_6_ = bf16[2304,512]{1,0:T(8,128)(2,1)S(1)} collective-permute-done((bf16[2304,512]{1,0:T(8,128)(2,1)}, bf16[2304,512]{1,0:T(8,128)(2,1)S(1)}, u32[]{:S(2)}, u32[]{:S(2)}) %collective-permute-start.7) | collective-permute-done | bytes 2359328 | tf_op jit(solution)/shard_map/ppermute | solution.py:34
  237.5 0.9 collective-permute-done.8.refs_7_
  238.9 16.6 %shard_map.71 = (bf16[2304,4096]{1,0:T(8,128)(2,1)}, f32[2304,128]{1,0:T(8,128)}, bf16[2304,384]{1,0:T(8,128)(2,1)}) custom-call(s32[8]{0:T(128)} %stack.35.starts_ref, bf16[2304,512]{1,0:T(8,128)(2,1)} %get-tuple-element.18.refs_8_.refs_0_, bf16[2304,512]{1,0:T(8,128)(2,1)} %collective-permute-done.3.refs_9_.refs_1_, ...), custom_call_target="tpu_custom_call" | custom-call | flops 4831838208 | bytes 37748736 | tf_op jit(solution)/shard_map/pallas_call | solution.py:224
  255.5 6.2 %all-gather.8.cloned.1.call-done.grads_ref = bf16[4096,3072]{1,0:T(8,128)(2,1)} async-done(((bf16[512,3072]{1,0:T(8,128)(2,1)}), bf16[4096,3072]{1,0:T(8,128)(2,1)}) %all-gather.8.cloned.1.call-update) | async-done | bytes 25165840 | tf_op jit(solution)/shard_map/all_gather | solution.py:362
  261.8 89.6 %shard_map.72 = (f32[256,4608]{1,0:T(8,128)}, f32[2304,4608]{1,0:T(8,128)}) custom-call(bf16[2304,4096]{1,0:T(8,128)(2,1)} %get-tuple-element.22.rows_ref, bf16[4096,3072]{1,0:T(8,128)(2,1)} %all-gather.8.cloned.1.call-done.grads_ref, bf16[2304,384]{1,0:T(8,128)(2,1)} %get-tuple-element.23.split_ref, bf16[256,4096]{1,0:T(8,128)(2,1)} %get-tuple-element.24.high_ref, ...), custom_call_target="tpu_custom_call" | custom-call | flops 76302778368 | bytes 72351744 | tf_op jit(solution)/shard_map/pallas_call | solution.py:303
  351.4 34.5 %shard_map.73 = (f32[256,4608]{1,0:T(8,128)}, f32[2304,4608]{1,0:T(8,128)}) custom-call(bf16[2304,4096]{1,0:T(8,128)(2,1)} %get-tuple-element.22.rows_ref, bf16[4096,1024]{1,0:T(8,128)(2,1)} %all-gather.6.cloned.1.call-done.grads_ref, bf16[2304,384]{1,0:T(8,128)(2,1)} %get-tuple-element.23.split_ref, ...), custom_call_target="tpu_custom_call", output_to_operand_aliasing={{0}: (6, {}), {1}: (7, {})} | custom-call | flops 25434259456 | bytes 36700160 | tf_op jit(solution)/shard_map/pallas_call | solution.py:303
  385.8 5.1 %all-gather.4.cloned.1.call-done.grads_ref = bf16[4096,512]{1,0:T(8,128)(2,1)} async-done(((bf16[512,512]{1,0:T(8,128)(2,1)}), bf16[4096,512]{1,0:T(8,128)(2,1)}) %all-gather.4.cloned.1.call-update) | async-done | bytes 4194320 | tf_op jit(solution)/shard_map/all_gather | solution.py:362
  391.0 19.2 %shard_map.74 = (f32[256,4608]{1,0:T(8,128)}, f32[2304,4608]{1,0:T(8,128)}) custom-call(bf16[2304,4096]{1,0:T(8,128)(2,1)} %get-tuple-element.22.rows_ref, bf16[4096,512]{1,0:T(8,128)(2,1)} %all-gather.4.cloned.1.call-done.grads_ref, bf16[2304,384]{1,0:T(8,128)(2,1)} %get-tuple-element.23.split_ref, ...), custom_call_target="tpu_custom_call", output_to_operand_aliasing={{0}: (6, {}), {1}: (7, {})} | custom-call | flops 12717129728 | bytes 27787264 | tf_op jit(solution)/shard_map/pallas_call | solution.py:303
  (62 shorter events, 8.6 us)
Async XLA Ops:
  7.2 33.3 %copy-start = (f32[256,2304]{1,0:T(8,128)S(1)}, f32[256,2304]{1,0:T(8,128)}, u32[]{:S(2)}) copy-start(f32[256,2304]{1,0:T(8,128)} %param.7) | copy-start | bytes 7077892
  7.2 254.6 %all-gather.8.cloned.1.call-start = ((), (), s32[]{:S(2)}) async-start(), calls=%async_computation.2 | async-start | bytes 28311552 | tf_op jit(solution)/shard_map/all_gather | solution.py:362
  11.2 340.2 %all-gather.6.cloned.1.call-start = ((), (), s32[]{:S(2)}) async-start(), calls=%async_computation.1 | async-start | bytes 9437184 | tf_op jit(solution)/shard_map/all_gather | solution.py:362
  13.5 377.5 %all-gather.4.cloned.1.call-start = ((), (), s32[]{:S(2)}) async-start(), calls=%async_computation | async-start | bytes 4718592 | tf_op jit(solution)/shard_map/all_gather | solution.py:362
  20.8 6.2 %collective-permute-start = (f32[128,128]{1,0:T(8,128)S(1)}, f32[128,128]{1,0:T(8,128)S(1)}, u32[]{:S(2)}, u32[]{:S(2)}) collective-permute-start(f32[128,128]{1,0:T(8,128)S(1)} %get-tuple-element.39), channel_id=1, source_target_pairs={{0,1},{1,2},{2,3},{3,0},{4,5},{5,6},{6,7},{7,4},{8,9},{9,10},{10,1... | collective-permute-start | bytes 196616 | tf_op jit(solution)/shard_map/ppermute | solution.py:34
  23.7 4.4 %collective-permute-start.1 = (f32[128,128]{1,0:T(8,128)S(1)}, f32[128,128]{1,0:T(8,128)S(1)}, u32[]{:S(2)}, u32[]{:S(2)}) collective-permute-start(f32[128,128]{1,0:T(8,128)S(1)} %get-tuple-element.38), channel_id=1, source_target_pairs={{0,2},{1,3},{2,0},{3,1},{4,6},{5,7},{6,4},{7,5},{8,10},{9,11},{10,... | collective-permute-start | bytes 196616 | tf_op jit(solution)/shard_map/ppermute | solution.py:34
  25.2 4.3 %collective-permute-start.2 = (f32[128,128]{1,0:T(8,128)S(1)}, f32[128,128]{1,0:T(8,128)S(1)}, u32[]{:S(2)}, u32[]{:S(2)}) collective-permute-start(f32[128,128]{1,0:T(8,128)S(1)} %get-tuple-element.37), channel_id=1, source_target_pairs={{0,3},{1,0},{2,1},{3,2},{4,7},{5,4},{6,5},{7,6},{8,11},{9,8},{10,9... | collective-permute-start | bytes 196616 | tf_op jit(solution)/shard_map/ppermute | solution.py:34
  27.0 2.5 copy-start.3
  28.2 1.3 copy-start.4
  29.5 0.6 copy-start.5
  36.4 56.4 %collective-permute-start.3 = (bf16[2304,512]{1,0:T(8,128)(2,1)}, bf16[2304,512]{1,0:T(8,128)(2,1)}, u32[]{:S(2)}, u32[]{:S(2)}) collective-permute-start(bf16[2304,512]{1,0:T(8,128)(2,1)} %get-tuple-element.18.refs_8_.refs_0_), channel_id=1, source_target_pairs={{0,1},{1,0},{2,3},{3,2},{4,5},{5,4},{6,7},{7,6},{8,9},{9,8},{10,11... | collective-permute-start | bytes 7077896 | tf_op jit(solution)/shard_map/ppermute | solution.py:34
  37.6 55.2 %collective-permute-start.4 = (bf16[2304,512]{1,0:T(8,128)(2,1)}, bf16[2304,512]{1,0:T(8,128)(2,1)}, u32[]{:S(2)}, u32[]{:S(2)}) collective-permute-start(bf16[2304,512]{1,0:T(8,128)(2,1)} %get-tuple-element.19.refs_10_.refs_2_), channel_id=1, source_target_pairs={{0,2},{2,0},{1,3},{3,1},{4,6},{6,4},{5,7},{7,5},{8,10},{10,8},{9,1... | collective-permute-start | bytes 7077896 | tf_op jit(solution)/shard_map/ppermute | solution.py:34
  39.4 101.0 %collective-permute-start.5 = (bf16[2304,512]{1,0:T(8,128)(2,1)}, bf16[2304,512]{1,0:T(8,128)(2,1)}, u32[]{:S(2)}, u32[]{:S(2)}) collective-permute-start(bf16[2304,512]{1,0:T(8,128)(2,1)} %get-tuple-element.18.refs_8_.refs_0_), channel_id=1, source_target_pairs={{0,2},{2,0},{1,3},{3,1},{4,6},{6,4},{5,7},{7,5},{8,10},{10,8},{9,1... | collective-permute-start | bytes 7077896 | tf_op jit(solution)/shard_map/ppermute | solution.py:34
  39.6 100.7 %collective-permute-start.6 = (bf16[2304,512]{1,0:T(8,128)(2,1)}, bf16[2304,512]{1,0:T(8,128)(2,1)}, u32[]{:S(2)}, u32[]{:S(2)}) collective-permute-start(bf16[2304,512]{1,0:T(8,128)(2,1)} %get-tuple-element.19.refs_10_.refs_2_), channel_id=1, source_target_pairs={{0,1},{1,0},{2,3},{3,2},{4,5},{5,4},{6,7},{7,6},{8,9},{9,8},{10,11... | collective-permute-start | bytes 7077896 | tf_op jit(solution)/shard_map/ppermute | solution.py:34
  46.5 2.3 collective-permute-start.9
  49.5 10.7 %collective-permute-start.10 = (f32[128,256]{1,0:T(8,128)S(1)}, f32[128,256]{1,0:T(8,128)S(1)}, u32[]{:S(2)}, u32[]{:S(2)}) collective-permute-start(f32[128,256]{1,0:T(8,128)S(1)} %get-tuple-element.35), channel_id=1, source_target_pairs={{0,8},{8,16},{16,24},{24,0},{1,9},{9,17},{17,25},{25,1},{2,10},{10... | collective-permute-start | bytes 393224 | tf_op jit(solution)/shard_map/ppermute | solution.py:34
  60.2 32.6 %copy-start.9 = (f32[128,256]{1,0:T(8,128)}, f32[128,256]{1,0:T(8,128)S(1)}, u32[]{:S(2)}) copy-start(f32[128,256]{1,0:T(8,128)S(1)} %collective-permute-done.10.refs_5_) | copy-start | bytes 393220
  60.2 22.6 %collective-permute-start.11 = (f32[128,256]{1,0:T(8,128)S(1)}, f32[128,256]{1,0:T(8,128)S(1)}, u32[]{:S(2)}, u32[]{:S(2)}) collective-permute-start(f32[128,256]{1,0:T(8,128)S(1)} %get-tuple-element.34), channel_id=1, source_target_pairs={{0,16},{8,24},{16,0},{24,8},{1,17},{9,25},{17,1},{25,9},{2,18},{10... | collective-permute-start | bytes 393224 | tf_op jit(solution)/shard_map/ppermute | solution.py:34
  82.8 10.0 %copy-start.10 = (f32[128,256]{1,0:T(8,128)}, f32[128,256]{1,0:T(8,128)S(1)}, u32[]{:S(2)}) copy-start(f32[128,256]{1,0:T(8,128)S(1)} %collective-permute-done.11.refs_6_) | copy-start | bytes 393220
  82.8 10.0 %collective-permute-start.12 = (f32[128,256]{1,0:T(8,128)S(1)}, f32[128,256]{1,0:T(8,128)S(1)}, u32[]{:S(2)}, u32[]{:S(2)}) collective-permute-start(f32[128,256]{1,0:T(8,128)S(1)} %get-tuple-element.33), channel_id=1, source_target_pairs={{0,24},{8,0},{16,8},{24,16},{1,25},{9,1},{17,9},{25,17},{2,26},{10... | collective-permute-start | bytes 393224 | tf_op jit(solution)/shard_map/ppermute | solution.py:34
  92.8 0.6 copy-start.11
  95.4 45.0 %collective-permute-start.13 = (f32[128,384]{1,0:T(8,128)}, f32[128,384]{1,0:T(8,128)S(1)}, u32[]{:S(2)}, u32[]{:S(2)}) collective-permute-start(f32[128,384]{1,0:T(8,128)} %shard_map.68.refs_0_), channel_id=1, source_target_pairs={{0,8},{8,16},{16,24},{24,0},{1,9},{9,17},{17,25},{25,1},{2,10},{10... | collective-permute-start | bytes 589832 | tf_op jit(solution)/shard_map/ppermute | solution.py:34
  100.8 39.6 %collective-permute-start.14 = (f32[128,384]{1,0:T(8,128)}, f32[128,384]{1,0:T(8,128)S(1)}, u32[]{:S(2)}, u32[]{:S(2)}) collective-permute-start(f32[128,384]{1,0:T(8,128)} %shard_map.68.refs_0_), channel_id=1, source_target_pairs={{0,16},{8,24},{16,0},{24,8},{1,17},{9,25},{17,1},{25,9},{2,18},{10... | collective-permute-start | bytes 589832 | tf_op jit(solution)/shard_map/ppermute | solution.py:34
  100.8 39.6 %collective-permute-start.15 = (f32[128,384]{1,0:T(8,128)}, f32[128,384]{1,0:T(8,128)S(1)}, u32[]{:S(2)}, u32[]{:S(2)}) collective-permute-start(f32[128,384]{1,0:T(8,128)} %shard_map.68.refs_0_), channel_id=1, source_target_pairs={{0,24},{8,0},{16,8},{24,16},{1,25},{9,1},{17,9},{25,17},{2,26},{10... | collective-permute-start | bytes 589832 | tf_op jit(solution)/shard_map/ppermute | solution.py:34
  140.3 0.7 copy-start.6
  140.4 0.7 copy-start.7
  141.1 0.7 copy-start.8
  143.9 21.6 %collective-permute-start.16 = (f32[512,384]{1,0:T(8,128)}, f32[512,384]{1,0:T(8,128)S(1)}, u32[]{:S(2)}, u32[]{:S(2)}) collective-permute-start(f32[512,384]{1,0:T(8,128)} %shard_map.69), channel_id=1, source_target_pairs={{0,1},{1,2},{2,3},{3,0},{4,5},{5,6},{6,7},{7,4},{8,9},{9,10},{10,1... | collective-permute-start | bytes 2359304 | tf_op jit(solution)/shard_map/ppermute | solution.py:34
  144.7 33.9 %collective-permute-start.17 = (f32[512,384]{1,0:T(8,128)}, f32[512,384]{1,0:T(8,128)S(1)}, u32[]{:S(2)}, u32[]{:S(2)}) collective-permute-start(f32[512,384]{1,0:T(8,128)} %shard_map.69), channel_id=1, source_target_pairs={{0,2},{1,3},{2,0},{3,1},{4,6},{5,7},{6,4},{7,5},{8,10},{9,11},{10,... | collective-permute-start | bytes 2359304 | tf_op jit(solution)/shard_map/ppermute | solution.py:34
  145.6 33.0 %collective-permute-start.18 = (f32[512,384]{1,0:T(8,128)}, f32[512,384]{1,0:T(8,128)S(1)}, u32[]{:S(2)}, u32[]{:S(2)}) collective-permute-start(f32[512,384]{1,0:T(8,128)} %shard_map.69), channel_id=1, source_target_pairs={{0,3},{1,0},{2,1},{3,2},{4,7},{5,4},{6,5},{7,6},{8,11},{9,8},{10,9... | collective-permute-start | bytes 2359304 | tf_op jit(solution)/shard_map/ppermute | solution.py:34
  181.6 6.9 %collective-permute-start.19 = (f32[2048,384]{1,0:T(8,128)}, f32[2048,384]{1,0:T(8,128)}, u32[]{:S(2)}, u32[]{:S(2)}) collective-permute-start(f32[2048,384]{1,0:T(8,128)} %pad_maximum_fusion.refs_0_), channel_id=1, source_target_pairs={{0,4},{4,0},{1,5},{5,1},{2,6},{6,2},{3,7},{7,3},{8,12},{12,8},{9,1... | collective-permute-start | bytes 9437192 | tf_op jit(solution)/shard_map/ppermute | solution.py:34
  183.6 53.9 %collective-permute-start.7 = (bf16[2304,512]{1,0:T(8,128)(2,1)}, bf16[2304,512]{1,0:T(8,128)(2,1)S(1)}, u32[]{:S(2)}, u32[]{:S(2)}) collective-permute-start(bf16[2304,512]{1,0:T(8,128)(2,1)} %collective-permute-done.3.refs_9_.refs_1_), channel_id=1, source_target_pairs={{0,2},{2,0},{1,3},{3,1},{4,6},{6,4},{5,7},{7,5},{8,10},{10,8},{9,1... | collective-permute-start | bytes 7077896 | tf_op jit(solution)/shard_map/ppermute | solution.py:34
  184.7 53.7 %collective-permute-start.8 = (bf16[2304,512]{1,0:T(8,128)(2,1)}, bf16[2304,512]{1,0:T(8,128)(2,1)}, u32[]{:S(2)}, u32[]{:S(2)}) collective-permute-start(bf16[2304,512]{1,0:T(8,128)(2,1)} %collective-permute-done.4.refs_11_.refs_3_), channel_id=1, source_target_pairs={{0,1},{1,0},{2,3},{3,2},{4,5},{5,4},{6,7},{7,6},{8,9},{9,8},{10,11... | collective-permute-start | bytes 7077896 | tf_op jit(solution)/shard_map/ppermute | solution.py:34
  237.5 1.4 copy-start.2
  391.0 19.2 %copy-start.1 = (f32[256,2304]{1,0:T(8,128)S(1)}, f32[256,2304]{1,0:T(8,128)}, u32[]{:S(2)}) copy-start(f32[256,2304]{1,0:T(8,128)} %param.7) | copy-start | bytes 7077892
Sparse Core Ops, SparseCore 0:
  11.3 250.4 all-gather.7
  263.4 80.2 all-gather.5
  345.3 45.6 all-gather.3
